TPU v7x, 32 devices: a whole 2x2x4 slice. The times are simulated.
32 devices in a mesh: dp: 16 (over z, y, x), tensor: 2 (over core).
Axes of the slice: x: 2, y: 2, z: 4, core: 2. Of those that a mesh axis runs over, the one named last changes fastest.
Arguments:
- inputs: bfloat16 [16384, 1024], P('dp'), may hold values from -6 to 6
- first_gain: float32 [1024], replicated, may hold values from 0.25 to 1.75
- query_weight: bfloat16 [1024, 1024], P(None, 'tensor'), may hold values from -0.1875 to 0.1875
- key_matrix: bfloat16 [1024, 512], P(None, 'tensor'), may hold values from -0.1875 to 0.1875
- value_matrix: bfloat16 [1024, 512], P(None, 'tensor'), may hold values from -0.1875 to 0.1875
- query_gain: float32 [64], replicated, may hold values from 0.25 to 1.75
- key_gain: float32 [64], replicated, may hold values from 0.25 to 1.75
- output_weight: bfloat16 [1024, 1024], P('tensor'), may hold values from -0.75 to 0.75
- second_gain: float32 [1024], replicated, may hold values from 0.25 to 1.75
- gate_weight: bfloat16 [1024, 4608], P(None, 'tensor'), may hold values from -0.1875 to 0.1875
- up_weight: bfloat16 [1024, 4608], P(None, 'tensor'), may hold values from -0.1875 to 0.1875
- down_weight: bfloat16 [4608, 1024], P('tensor'), may hold values from -0.09375 to 0.09375
- cotangent: bfloat16 [16384, 1024], P('dp'), may hold values from -6 to 6
Outputs:
- result: bfloat16 [16384, 1024], P('dp')
- input_grad: float32 [16384, 1024], P('dp')
- first_gain_grad: float32 [1024], P('dp')
- query_weight_grad: float32 [1024, 1024], P('dp', 'tensor')
- key_weight_grad: float32 [1024, 512], P('dp', 'tensor')
- value_weight_grad: float32 [1024, 512], P('dp', 'tensor')
- query_gain_grad: float32 [64], replicated
- key_gain_grad: float32 [64], replicated
- output_weight_grad: float32 [1024, 1024], P('tensor', 'dp')
- second_gain_grad: float32 [1024], P('dp')
- gate_weight_grad: float32 [1024, 4608], P('dp', 'tensor')
- up_weight_grad: float32 [1024, 4608], P('dp', 'tensor')
- down_weight_grad: float32 [4608, 1024], P('tensor', 'dp')
All inputs are finite; a program needn't handle non-finite values.
Results may differ from a plain program's by a relative error of at most 0.014.
Values sent between devices are 32-bit elements; how exact they have to be, the bound alone decides.
No kernel may reach another device: no remote copies, remote signals or barrier semaphores. Data moves between devices by JAX's collectives and lax.ppermute only.
A program may use at most 192 MiB of HBM per device.

v0:
```python
import math

import jax
import jax.numpy as jnp
from jax import lax
from jax.sharding import PartitionSpec as P

EPSILON = 1e-05
ROPE_BASE = 1000000.0
MASKED = -1e30


def rms_scale(values, gain):
    return values * lax.rsqrt(jnp.mean(values * values, axis=-1, keepdims=True) + EPSILON) * gain


def rope_tables(length, width):
    half_width = width // 2
    frequency = jnp.exp(
        jnp.arange(half_width, dtype=jnp.float32) * (-2.0 * math.log(ROPE_BASE) / width)
    )
    angles = jnp.arange(length, dtype=jnp.float32)[:, None] * frequency[None, :]
    angles = jnp.concatenate([angles, angles], axis=1)
    return (jnp.cos(angles)[:, None, :], jnp.sin(angles)[:, None, :])


def rotate(values, cosine_table, sine_table):
    half_width = values.shape[-1] // 2
    turned = jnp.concatenate([-values[..., half_width:], values[..., :half_width]], axis=-1)
    return values * cosine_table + turned * sine_table


def swiglu(gate_in, up_in):
    return jax.nn.silu(gate_in) * up_in


def contract_rows(left_side, right_side):
    return lax.dot_general(
        left_side, right_side, (((0,), (0,)), ((), ())), preferred_element_type=jnp.float32
    )


def contract_cols(left_side, right_side):
    return lax.dot_general(
        left_side, right_side, (((1,), (1,)), ((), ())), preferred_element_type=jnp.float32
    )


def local(
    inputs,
    first_gain,
    query_weight,
    key_matrix,
    value_matrix,
    query_gain,
    key_gain,
    output_weight,
    second_gain,
    gate_weight,
    up_weight,
    down_weight,
    cotangent,
):
    row_count = inputs.shape[0]
    head_dim = query_gain.shape[0]
    groups = key_matrix.shape[1] // head_dim
    repeat = query_weight.shape[1] // key_matrix.shape[1]
    score_scale = head_dim ** (-0.5)
    block_rows = min(512, row_count)
    cosine_table, sine_table = rope_tables(row_count, head_dim)

    def shape_heads(projected, gain):
        return rotate(
            rms_scale(projected.reshape(row_count, -1, head_dim), gain), cosine_table, sine_table
        )

    source = inputs.astype(jnp.float32)
    first_normed, first_pull = jax.vjp(rms_scale, source, first_gain)
    normalized_input = first_normed.astype(jnp.bfloat16)
    query_proj = jnp.dot(normalized_input, query_weight, preferred_element_type=jnp.float32)
    projected_key = jnp.dot(normalized_input, key_matrix, preferred_element_type=jnp.float32)
    reduced_value = (
        jnp.dot(normalized_input, value_matrix, preferred_element_type=jnp.float32)
        .astype(jnp.bfloat16)
        .reshape(row_count, groups, head_dim)
    )
    query_turned, query_pull = jax.vjp(shape_heads, query_proj, query_gain)
    key_turned, key_pull = jax.vjp(shape_heads, projected_key, key_gain)
    reduced_query = query_turned.astype(jnp.bfloat16).reshape(row_count, groups, repeat, head_dim)
    key_low = key_turned.astype(jnp.bfloat16)

    def block_scores(row_start, row_end):
        scores = (
            jnp.einsum(
                "qgrd,kgd->grqk",
                reduced_query[row_start:row_end],
                key_low[:row_end],
                preferred_element_type=jnp.float32,
            )
            * score_scale
        )
        causal = jnp.arange(row_start, row_end)[:, None] >= jnp.arange(row_end)[None, :]
        return jnp.where(causal, scores, MASKED)

    pieces = []
    totals = []
    for row_start in range(0, row_count, block_rows):
        row_end = row_start + block_rows
        scores = block_scores(row_start, row_end)
        highest = jnp.max(scores, axis=-1, keepdims=True)
        weights = jnp.exp(scores - highest)
        row_total = jnp.sum(weights, axis=-1, keepdims=True)
        probabilities = (weights / row_total).astype(jnp.bfloat16)
        pieces.append(
            jnp.einsum(
                "grqk,kgd->qgrd",
                probabilities,
                reduced_value[:row_end],
                preferred_element_type=jnp.float32,
            )
        )
        totals.append(highest + jnp.log(row_total))
    mixed = jnp.concatenate(pieces, axis=0).reshape(row_count, -1).astype(jnp.bfloat16)
    attention = lax.psum(
        jnp.dot(mixed, output_weight, preferred_element_type=jnp.float32), "tensor"
    )
    middle = source + attention
    second_normed, second_pull = jax.vjp(rms_scale, middle, second_gain)
    normed_mid = second_normed.astype(jnp.bfloat16)
    gate_act = jnp.dot(normed_mid, gate_weight, preferred_element_type=jnp.float32)
    up_act = jnp.dot(normed_mid, up_weight, preferred_element_type=jnp.float32)
    activated, act_pull = jax.vjp(swiglu, gate_act, up_act)
    hidden = activated.astype(jnp.bfloat16)
    branch = lax.psum(jnp.dot(hidden, down_weight, preferred_element_type=jnp.float32), "tensor")
    result = (middle + branch).astype(jnp.bfloat16)
    down_grad = contract_rows(hidden, cotangent)
    hidden_back = contract_cols(cotangent, down_weight)
    gate_back, up_back = act_pull(hidden_back)
    gate_back = gate_back.astype(jnp.bfloat16)
    up_back = up_back.astype(jnp.bfloat16)
    gate_grad = contract_rows(normed_mid, gate_back)
    up_grad = contract_rows(normed_mid, up_back)
    mid_partial = contract_cols(gate_back, gate_weight) + contract_cols(up_back, up_weight)
    mid_back = lax.psum(mid_partial, "tensor")
    middle_norm_back, second_gain_grad = second_pull(mid_back)
    middle_grad = cotangent.astype(jnp.float32) + middle_norm_back
    attention_back = middle_grad.astype(jnp.bfloat16)
    output_grad = contract_rows(mixed, attention_back)
    mixed_back = (
        contract_cols(attention_back, output_weight)
        .astype(jnp.bfloat16)
        .reshape(row_count, groups, repeat, head_dim)
    )
    key_accum = jnp.zeros((row_count, groups, head_dim), jnp.float32)
    value_accum = jnp.zeros((row_count, groups, head_dim), jnp.float32)
    query_parts = []
    for block_index, row_start in enumerate(range(0, row_count, block_rows)):
        row_end = row_start + block_rows
        scores = block_scores(row_start, row_end)
        probabilities = jnp.exp(scores - totals[block_index])
        incoming = mixed_back[row_start:row_end]
        prob_back = jnp.einsum(
            "qgrd,kgd->grqk", incoming, reduced_value[:row_end], preferred_element_type=jnp.float32
        )
        value_accum = value_accum.at[:row_end].add(
            jnp.einsum(
                "grqk,qgrd->kgd",
                probabilities.astype(jnp.bfloat16),
                incoming,
                preferred_element_type=jnp.float32,
            )
        )
        score_back = (
            probabilities * (prob_back - jnp.sum(probabilities * prob_back, axis=-1, keepdims=True))
        ).astype(jnp.bfloat16)
        query_parts.append(
            jnp.einsum(
                "grqk,kgd->qgrd", score_back, key_low[:row_end], preferred_element_type=jnp.float32
            )
            * score_scale
        )
        key_accum = key_accum.at[:row_end].add(
            jnp.einsum(
                "grqk,qgrd->kgd",
                score_back,
                reduced_query[row_start:row_end],
                preferred_element_type=jnp.float32,
            )
            * score_scale
        )
    query_rot_back = jnp.concatenate(query_parts, axis=0).reshape(
        row_count, groups * repeat, head_dim
    )
    query_proj_back, query_gain_part = query_pull(query_rot_back)
    key_proj_back, key_gain_part = key_pull(key_accum)
    query_back = query_proj_back.astype(jnp.bfloat16)
    key_back = key_proj_back.astype(jnp.bfloat16)
    value_back = value_accum.reshape(row_count, -1).astype(jnp.bfloat16)
    query_grad = contract_rows(normalized_input, query_back)
    key_grad = contract_rows(normalized_input, key_back)
    value_grad = contract_rows(normalized_input, value_back)
    normed_partial = (
        contract_cols(query_back, query_weight)
        + contract_cols(key_back, key_matrix)
        + contract_cols(value_back, value_matrix)
    )
    normed_back = lax.psum(normed_partial, "tensor")
    source_back, first_gain_grad = first_pull(normed_back)
    input_grad = middle_grad + source_back
    query_gain_grad, key_gain_grad = lax.psum((query_gain_part, key_gain_part), ("dp", "tensor"))
    (
        first_shard,
        query_shard,
        key_shard,
        value_shard,
        output_shard,
        second_shard,
        gate_shard,
        up_shard,
        down_shard,
    ) = (
        lax.psum_scatter(first_gain_grad, "dp", scatter_dimension=0, tiled=True),
        lax.psum_scatter(query_grad, "dp", scatter_dimension=0, tiled=True),
        lax.psum_scatter(key_grad, "dp", scatter_dimension=0, tiled=True),
        lax.psum_scatter(value_grad, "dp", scatter_dimension=0, tiled=True),
        lax.psum_scatter(output_grad, "dp", scatter_dimension=1, tiled=True),
        lax.psum_scatter(second_gain_grad, "dp", scatter_dimension=0, tiled=True),
        lax.psum_scatter(gate_grad, "dp", scatter_dimension=0, tiled=True),
        lax.psum_scatter(up_grad, "dp", scatter_dimension=0, tiled=True),
        lax.psum_scatter(down_grad, "dp", scatter_dimension=1, tiled=True),
    )
    return (
        result,
        input_grad,
        first_shard,
        query_shard,
        key_shard,
        value_shard,
        query_gain_grad,
        key_gain_grad,
        output_shard,
        second_shard,
        gate_shard,
        up_shard,
        down_shard,
    )


def solution(mesh):
    placed = (
        P("dp", None),
        P(),
        P(None, "tensor"),
        P(None, "tensor"),
        P(None, "tensor"),
        P(),
        P(),
        P("tensor", None),
        P(),
        P(None, "tensor"),
        P(None, "tensor"),
        P("tensor", None),
        P("dp", None),
    )
    return jax.shard_map(
        local,
        mesh=mesh,
        in_specs=placed,
        out_specs=(
            P("dp", None),
            P("dp", None),
            P("dp"),
            P("dp", "tensor"),
            P("dp", "tensor"),
            P("dp", "tensor"),
            P(),
            P(),
            P("tensor", "dp"),
            P("dp"),
            P("dp", "tensor"),
            P("dp", "tensor"),
            P("tensor", "dp"),
        ),
        check_vma=False,
    )
```

profile of v0, /device:TPU:0, one launch (start us, length us, event | category | flops | bytes accessed | tf_op | source)
XLA Modules:
  0.0 1138.7 jit_solution(15207796097090551737)
XLA Ops:
  7.4 2.2 fusion.26
  10.3 1.0 fusion.67
  11.7 2.6 convolution_convert_fusion.1
  14.4 0.9 multiply_reduce_fusion.8
  15.7 1.4 multiply_reduce_fusion.5
  18.5 0.7 fusion.32
  19.8 1.5 fusion.89
  21.3 1.2 fusion.16
  22.5 2.1 copy-done.1
  24.6 1.6 fusion.57
  26.2 7.8 fusion.88
  34.0 8.0 fusion.3
  42.0 7.5 fusion.56
  49.6 1.0 copy-done.16
  50.6 3.3 fusion.90
  54.0 31.2 %all-reduce.15.cloned.1.call-done = f32[1024,1024]{1,0:T(8,128)} async-done(((f32[1024,1024]{1,0:T(8,128)}), f32[1024,1024]{1,0:T(8,128)}) %all-reduce.15.cloned.1.call-update) | async-done | bytes 4194320 | tf_op jit(solution)/shard_map/psum | solution.py:124
  85.2 2.8 multiply_reduce_fusion.2
  88.5 12.1 %fusion.92 = f32[1024,2304]{1,0:T(8,128)} fusion(bf16[1024,1024]{1,0:T(8,128)(2,1)S(1)} %multiply_convert_fusion.2, bf16[1024,2304]{1,0:T(8,128)(2,1)} %param.35), kind=kOutput, calls=%fused_computation.150 | convolution fusion | flops 4831838208 | bytes 16252928 | tf_op jit(solution)/shard_map/dot_general | solution.py:131
  100.7 7.4 fusion.91
  108.1 18.2 %multiply_convert_fusion = (bf16[1024,2304]{1,0:T(8,128)(2,1)}, bf16[1024,2304]{1,0:T(8,128)(2,1)}, bf16[1024,2304]{1,0:T(8,128)(2,1)}) fusion(f32[1024,2304]{1,0:T(8,128)} %fusion.91, f32[1024,2304]{1,0:T(8,128)} %fusion.92, bf16[1024,1024]{1,0:T(8,128)(2,1)S(1)} %copy-done.31, bf16[2304,1024]{1,0:T(8,128)(2,1)} %param.36), kind=kOutput, calls=%fused_computation.15 | convolution fusion | flops 4869586944 | bytes 39845888 | tf_op jit(solution)/shard_map/dot_general | solution.py:44
  126.3 8.5 fusion.94
  134.8 9.1 convolution_add_fusion
  144.0 9.8 fusion.93
  153.8 19.9 %all-reduce.17.cloned.1.call-done = f32[1024,1024]{1,0:T(8,128)} async-done(((f32[1024,1024]{1,0:T(8,128)}), f32[1024,1024]{1,0:T(8,128)}) %all-reduce.17.cloned.1.call-update) | async-done | bytes 4194320 | tf_op jit(solution)/shard_map/psum | solution.py:144
  173.7 4.6 multiply_reduce_fusion
  178.3 3.3 fusion.22
  181.6 1.3 convolution_convert_fusion
  183.7 2.2 fusion.51
  185.9 5.1 fusion.11
  191.1 4.8 fusion.13
  195.9 2.2 fusion.55
  198.1 1.8 fusion.42
  200.1 8.1 fusion
  208.2 4.0 fusion.46
  212.3 2.0 fusion.96
  214.3 8.3 fusion.2
  222.6 3.3 copy-done.4
  225.9 1.5 fusion.41
  227.5 6.1 broadcast_multiply_fusion
  235.5 1.1 copy-done.6
  236.6 1.5 multiply_reduce_fusion.3
  238.4 0.8 fusion.95
  239.9 1.0 copy-done.23
  240.8 3.3 add_add_fusion.2
  244.2 1.5 copy-done.10
  245.7 3.0 fusion.72
  248.8 3.0 fusion.74
  252.3 5.9 fusion.61
  258.3 4.3 fusion.76
  262.7 10.3 fusion.99
  273.1 10.8 fusion.98
  283.9 10.2 fusion.97
  295.9 40.8 %all-reduce.8 = (f32[64]{0:T(128)}, f32[64]{0:T(128)}) all-reduce(f32[64]{0:T(128)S(1)} %get-tuple-element.81, f32[64]{0:T(128)S(1)} %get-tuple-element.83), channel_id=1, replica_groups=mesh['dp'=16,'tensor'=2] {'dp','tensor'}, use_global_device_ids=true, to_apply=%region_24.25 | all-reduce | flops 128 | bytes 1024 | tf_op jit(solution)/shard_map/psum | solution.py:210
  336.7 3.6 fusion.21
  340.3 41.3 %all-reduce.9 = (f32[1024]{0:T(1024)S(1)}, f32[1024]{0:T(1024)S(1)}) all-reduce(f32[1024]{0:T(1024)S(1)} %get-tuple-element.79, f32[1024]{0:T(1024)S(1)} %get-tuple-element.77), channel_id=2, replica_groups=mesh['dp'=16,'tensor'=2] {'dp'}, use_global_device_ids=true, to_apply=%region_19.20.clone | all-reduce | flops 2048 | bytes 16384
  382.8 5.7 add_convert_fusion
  388.5 1.0 copy-done.15
  389.5 2.6 fusion.23
  392.1 51.0 %reduce-scatter.10.cloned.1.call-done = f32[64,256]{1,0:T(8,128)} async-done(((f32[1024,256]{1,0:T(8,128)}), f32[64,256]{1,0:T(8,128)}) %reduce-scatter.10.cloned.1.call-update) | async-done | bytes 65552 | tf_op jit(solution)/shard_map/reduce_scatter | solution.py:224
  443.2 79.6 %reduce-scatter.14.cloned.1.call-done = f32[512,64]{0,1:T(8,128)} async-done(((f32[512,1024]{0,1:T(8,128)}), f32[512,64]{0,1:T(8,128)}) %reduce-scatter.14.cloned.1.call-update) | async-done | bytes 131088 | tf_op jit(solution)/shard_map/reduce_scatter | solution.py:226
  522.8 81.2 %reduce-scatter.8.cloned.1.call-done = f32[64,512]{1,0:T(8,128)} async-done(((f32[1024,512]{1,0:T(8,128)}), f32[64,512]{1,0:T(8,128)}) %reduce-scatter.8.cloned.1.call-update) | async-done | bytes 131088 | tf_op jit(solution)/shard_map/reduce_scatter | solution.py:223
  604.0 174.4 %reduce-scatter.20.cloned.1.call-done = f32[2304,64]{0,1:T(8,128)} async-done(((f32[2304,1024]{0,1:T(8,128)}), f32[2304,64]{0,1:T(8,128)}) %reduce-scatter.20.cloned.1.call-update) | async-done | bytes 589840 | tf_op jit(solution)/shard_map/reduce_scatter | solution.py:230
  778.4 177.1 %reduce-scatter.18.cloned.1.call-done = f32[64,2304]{1,0:T(8,128)} async-done(((f32[1024,2304]{1,0:T(8,128)}), f32[64,2304]{1,0:T(8,128)}) %reduce-scatter.18.cloned.1.call-update) | async-done | bytes 589840 | tf_op jit(solution)/shard_map/reduce_scatter | solution.py:229
  955.5 176.2 %reduce-scatter.16.cloned.1.call-done = f32[64,2304]{1,0:T(8,128)} async-done(((f32[1024,2304]{1,0:T(8,128)}), f32[64,2304]{1,0:T(8,128)}) %reduce-scatter.16.cloned.1.call-update) | async-done | bytes 589840 | tf_op jit(solution)/shard_map/reduce_scatter | solution.py:228
  (189 shorter events, 11.1 us)
Async XLA Ops:
  7.2 8.5 copy-start
  7.2 78.0 %all-reduce.15.cloned.1.call-start = ((), (), s32[]{:S(2)}) async-start(), calls=%async_computation.7 | async-start | bytes 8388608 | tf_op jit(solution)/shard_map/psum | solution.py:124
  7.4 7.0 copy-start.9
  7.4 7.0 copy-start.38
  7.4 7.0 copy-start.52
  10.2 5.5 copy-start.50
  11.3 8.1 copy-start.13
  11.3 8.1 copy-start.19
  14.3 27.7 %copy-start.32 = (bf16[1024,256]{0,1:T(8,128)(2,1)}, bf16[1024,256]{0,1:T(8,128)(2,1)S(1)}, u32[]{:S(2)}) copy-start(bf16[1024,256]{0,1:T(8,128)(2,1)S(1)} %convolution_convert_fusion.1) | copy-start | bytes 1572868
  15.3 1.9 copy-start.45
  15.3 4.0 copy-start.11
  15.3 4.0 copy-start.40
  19.3 2.0 copy-start.17
  19.3 6.9 copy-start.28
  19.8 6.4 copy-start.21
  21.3 3.3 copy-start.1
  42.0 8.6 copy-start.34
  53.9 34.1 %copy-start.49 = (f32[1024]{0:T(1024)S(1)}, f32[1024]{0:T(1024)}, u32[]{:S(2)}) copy-start(f32[1024]{0:T(1024)} %param.33) | copy-start | bytes 12292
  54.0 119.7 %all-reduce.17.cloned.1.call-start = ((), (), s32[]{:S(2)}) async-start(), calls=%async_computation.8 | async-start | bytes 8388608 | tf_op jit(solution)/shard_map/psum | solution.py:144
  88.0 12.6 %copy-start.2 = (f32[1024,1024]{1,0:T(8,128)}, f32[1024,1024]{1,0:T(8,128)S(1)}, u32[]{:S(2)}) copy-start(f32[1024,1024]{1,0:T(8,128)S(1)} %get-tuple-element.94) | copy-start | bytes 12582916
  88.0 12.6 %slice-start.6 = ((s8[4718592]{0:T(1024)(128)(4,1)}), s8[4194304]{0:T(1024)(128)(4,1)S(1)}, s32[]{:S(2)}) async-start(s8[4718592]{0:T(1024)(128)(4,1)} %bitcast.216), calls=%async_computation.23 | async-start | bytes 8388608
  88.5 12.2 %copy-start.27 = (bf16[1024,1024]{1,0:T(8,128)(2,1)}, bf16[1024,1024]{1,0:T(8,128)(2,1)S(1)}, u32[]{:S(2)}) copy-start(bf16[1024,1024]{1,0:T(8,128)(2,1)S(1)} %multiply_convert_fusion.2) | copy-start | bytes 6291460
  88.5 12.2 %slice-start.7 = ((s8[4718592]{0:T(1024)(128)(4,1)}), s8[524288]{0:T(1024)(128)(4,1)S(1)}, s32[]{:S(2)}) async-start(s8[4718592]{0:T(1024)(128)(4,1)} %bitcast.216), calls=%async_computation.24 | async-start | bytes 1048576
  100.7 7.4 copy-start.31
  126.3 8.5 copy-start.59
  143.9 192.9 %all-reduce.19.cloned.1.call-start = ((), (), s32[]{:S(2)}) async-start(), calls=%async_computation.16 | async-start | bytes 16777216 | tf_op jit(solution)/shard_map/psum | solution.py:134
  173.7 4.6 copy-start.3
  173.7 10.0 slice-start.4
  178.3 3.3 copy-start.35
  178.3 5.3 slice-start.5
  181.6 2.0 copy-start.7
  191.0 4.9 copy-start.18
  191.0 8.9 slice-start
  191.0 8.9 slice-start.1
  191.0 8.9 slice-start.2
  195.9 2.2 copy-start.22
  195.9 4.2 slice-start.3
  198.1 2.0 copy-start.33
  212.2 10.3 copy-start.25
  212.3 2.0 copy-start.44
  222.6 3.3 copy-start.4
  225.9 1.6 copy-start.26
  225.9 1.6 copy-start.29
  227.4 6.3 copy-start.12
  227.4 6.3 copy-start.20
  227.5 6.3 copy-start.41
  227.5 6.3 copy-start.57
  235.0 1.6 copy-start.6
  235.0 1.6 copy-start.37
  235.0 1.6 copy-start.55
  236.6 1.8 copy-start.39
  244.1 1.6 copy-start.10
  244.1 1.6 copy-start.51
  244.1 1.6 copy-start.53
  244.1 148.0 %reduce-scatter.12.cloned.1.call-start = ((), (), s32[]{:S(2)}) async-start(), calls=%async_computation.11 | async-start | bytes 1114112 | tf_op jit(solution)/shard_map/reduce_scatter | solution.py:225
  248.7 194.4 %reduce-scatter.10.cloned.1.call-start = ((), (), s32[]{:S(2)}) async-start(), calls=%async_computation.10 | async-start | bytes 1114112 | tf_op jit(solution)/shard_map/reduce_scatter | solution.py:224
  251.8 271.0 %reduce-scatter.14.cloned.1.call-start = ((), (), s32[]{:S(2)}) async-start(), calls=%async_computation.12 | async-start | bytes 2228224 | tf_op jit(solution)/shard_map/reduce_scatter | solution.py:226
  258.2 345.8 %reduce-scatter.8.cloned.1.call-start = ((), (), s32[]{:S(2)}) async-start(), calls=%async_computation.9 | async-start | bytes 2228224 | tf_op jit(solution)/shard_map/reduce_scatter | solution.py:223
  262.7 515.7 %reduce-scatter.20.cloned.1.call-start = ((), (), s32[]{:S(2)}) async-start(), calls=%async_computation.15 | async-start | bytes 10027008 | tf_op jit(solution)/shard_map/reduce_scatter | solution.py:230
  273.0 682.5 %reduce-scatter.18.cloned.1.call-start = ((), (), s32[]{:S(2)}) async-start(), calls=%async_computation.14 | async-start | bytes 10027008 | tf_op jit(solution)/shard_map/reduce_scatter | solution.py:229
  283.8 847.9 %reduce-scatter.16.cloned.1.call-start = ((), (), s32[]{:S(2)}) async-start(), calls=%async_computation.13 | async-start | bytes 10027008 | tf_op jit(solution)/shard_map/reduce_scatter | solution.py:228
  294.1 88.7 %copy-start.48 = (f32[1024]{0:T(1024)S(1)}, f32[1024]{0:T(1024)}, u32[]{:S(2)}) copy-start(f32[1024]{0:T(1024)} %copy-done.47) | copy-start | bytes 12292
  382.8 5.7 copy-start.8
  382.8 6.7 copy-start.15
  (14 other events, 15.6 us)
Sparse Core Ops, SparseCore 0:
  54.1 31.1 all-reduce.14
  144.0 29.6 all-reduce.16
  244.3 40.0 all-reduce.18
  287.1 79.0 reduce-scatter.11
  368.9 74.2 reduce-scatter.9
  445.9 76.8 reduce-scatter.13
  525.7 78.2 reduce-scatter.7
  610.2 168.1 reduce-scatter.19
  785.6 169.8 reduce-scatter.17
  961.6 170.0 reduce-scatter.15
where the time goes:
time: 1150 us; the launch traced here: 1140 us
  waiting for transfers between devices  791 us (69%)
  matrix products  178 us (15%)
  blocking collectives  82.1 us (7%)
  other arithmetic  55 us (5%)
  local copies, waits for them, and re-layouts  16.2 us (1%)
  between operations  16.1 us (1%)
    reduce_scatter x1, waiting for transfers between devices, local(): lax.psum_scatter(up_grad, 'dp', scatter_dimension=0, tiled=True)  177 us
    reduce_scatter x1, waiting for transfers between devices, local(): lax.psum_scatter(gate_grad, 'dp', scatter_dimension=0, tiled=True)  176 us
    reduce_scatter x1, waiting for transfers between devices, local(): lax.psum_scatter(down_grad, 'dp', scatter_dimension=1, tiled=True)  174 us
    reduce_scatter x1, waiting for transfers between devices, local(): lax.psum_scatter(query_grad, 'dp', scatter_dimension=0, tiled=True)  81.2 us
    reduce_scatter x1, waiting for transfers between devices, local(): lax.psum_scatter(output_grad, 'dp', scatter_dimension=1, tiled=True)  79.6 us
    reduce_scatter x1, waiting for transfers between devices, local(): lax.psum_scatter(key_grad, 'dp', scatter_dimension=0, tiled=True)  51 us
    dot_general x7, matrix products, contract_rows(): lax.dot_general(left_side, right_side, (((0,), (0,)), ((), ())), preferre...  47.5 us
    dot_general x7, matrix products, contract_cols(): lax.dot_general(left_side, right_side, (((1,), (1,)), ((), ())), preferre...  43.1 us
  transfers between devices with their start and end apart: 10, of which 8 were waited for; matrix products, arithmetic and copies ran while one was open for 6% of the time, Pallas kernels for 0%

commit v1 on v0

v1 whole, which is shorter than its diff:
```python
import functools
import math

import jax
import jax.numpy as jnp
from jax import lax
from jax.experimental import pallas as pl
from jax.experimental.pallas import tpu as pltpu
from jax.sharding import Mesh, PartitionSpec as P

EPSILON = 1e-05
ROPE_BASE = 1000000.0
BLOCK = 256
VMEM_LIMIT = 60 * 1024 * 1024
SWAP = [(0, 1), (1, 0)]
SHIFT = 8.0


def rms_scale(values, gain):
    return values * lax.rsqrt(jnp.mean(values * values, axis=-1, keepdims=True) + EPSILON) * gain


def rope_tables(length, width):
    half_width = width // 2
    frequency = jnp.exp(
        jnp.arange(half_width, dtype=jnp.float32) * (-2.0 * math.log(ROPE_BASE) / width)
    )
    angles = jnp.arange(length, dtype=jnp.float32)[None, :] * frequency[:, None]
    angles = jnp.concatenate([angles, angles], axis=0)
    return jnp.cos(angles), jnp.sin(angles)


def head_forward(values, gain, cosine, sine):
    scale = lax.rsqrt(jnp.mean(values * values, axis=0, keepdims=True) + EPSILON)
    normed = values * scale * gain
    half_width = values.shape[0] // 2
    turned = jnp.concatenate([-normed[half_width:], normed[:half_width]], axis=0)
    return normed * cosine + turned * sine


def head_backward(values, gain, cosine, sine, grad):
    half_width = values.shape[0] // 2
    crossed = grad * sine
    back = grad * cosine + jnp.concatenate([crossed[half_width:], -crossed[:half_width]], axis=0)
    scale = lax.rsqrt(jnp.mean(values * values, axis=0, keepdims=True) + EPSILON)
    hat = values * scale
    scaled = back * gain
    out = scale * (scaled - hat * jnp.mean(scaled * hat, axis=0, keepdims=True))
    return out, fold_lanes(back * hat)


def fold_lanes(values):
    total = values[:, :128]
    for at in range(128, values.shape[1], 128):
        total = total + values[:, at : at + 128]
    return total


def visible(size):
    key = lax.broadcasted_iota(jnp.int32, (size, size), 0)
    query = lax.broadcasted_iota(jnp.int32, (size, size), 1)
    return key <= query


def dot32(left, right):
    return jnp.dot(left, right, preferred_element_type=jnp.float32)


def attend_kernel(
    query_ref, key_ref, value_ref, query_gain_ref, key_gain_ref, cosine_ref, sine_ref,
    mixed_ref, query_low_ref, key_low_ref, value_low_ref, total_ref,
):
    width, length = key_ref.shape
    repeat = query_ref.shape[0] // width
    score_scale = width ** (-0.5)
    cosine, sine = cosine_ref[...], sine_ref[...]
    key = head_forward(key_ref[...], key_gain_ref[...], cosine, sine)
    key_low_ref[...] = key.astype(jnp.bfloat16)
    key_rows = key.T.astype(jnp.bfloat16)
    value_low = value_ref[...].astype(jnp.bfloat16)
    value_low_ref[...] = value_low
    ones = jnp.ones((16, length), jnp.bfloat16)
    value_and_one = jnp.concatenate([value_low, ones], axis=0)
    mask = visible(BLOCK)
    for head in range(repeat):
        at = slice(head * width, (head + 1) * width)
        query = head_forward(query_ref[at, :], query_gain_ref[...], cosine, sine)
        query_low = (query.astype(jnp.bfloat16).astype(jnp.float32) * score_scale).astype(
            jnp.bfloat16
        )
        query_low_ref[at, :] = query_low
        for start in range(0, length, BLOCK):
            stop = start + BLOCK
            columns = query_low[:, start:stop]
            near = jnp.exp(dot32(key_rows[start:stop], columns))
            near = jnp.where(mask, near, 0.0).astype(jnp.bfloat16)
            out = dot32(value_and_one[:, start:stop], near)
            if start:
                far = jnp.exp(dot32(key_rows[:start], columns)).astype(jnp.bfloat16)
                out = out + dot32(value_and_one[:, :start], far)
            total = out[width : width + 1]
            mixed_ref[at, start:stop] = (out[:width] / total).astype(jnp.bfloat16)
            total_ref[head : head + 1, start:stop] = jnp.log(total)


def attend_back_kernel(
    query_ref, key_ref, query_gain_ref, key_gain_ref, cosine_ref, sine_ref,
    query_low_ref, key_low_ref, value_low_ref, mixed_ref, total_ref, back_ref,
    query_back_ref, key_back_ref, value_back_ref, query_part_ref, key_part_ref,
    key_sum, value_sum,
):
    width, length = key_ref.shape
    repeat = query_ref.shape[0] // width
    score_scale = width ** (-0.5)
    cosine, sine = cosine_ref[...], sine_ref[...]

    def rows_of(value):
        return value.astype(jnp.float32).T.astype(jnp.bfloat16)

    key_low = key_low_ref[...]
    key_rows = rows_of(key_low)
    value_rows = rows_of(value_low_ref[...])
    mask = visible(BLOCK)
    key_sum[...] = jnp.zeros_like(key_sum)
    value_sum[...] = jnp.zeros_like(value_sum)
    query_part = jnp.zeros((width, 128), jnp.float32)
    for head in range(repeat):
        at = slice(head * width, (head + 1) * width)
        query_low = query_low_ref[at, :]
        query_rows = rows_of(query_low)
        back = back_ref[at, :]
        back_rows = rows_of(back)
        delta = jnp.sum(
            mixed_ref[at, :].astype(jnp.float32) * back.astype(jnp.float32), axis=0, keepdims=True
        )
        total = total_ref[head : head + 1, :]
        grads = []
        for start in range(0, length, BLOCK):
            stop = start + BLOCK
            columns, incoming = query_low[:, start:stop], back[:, start:stop]
            shift, inner = total[:, start:stop], delta[:, start:stop]
            grad = None
            for low, high in ((start, stop), (0, start)):
                if low == high:
                    continue
                weights = jnp.exp(dot32(key_rows[low:high], columns) - shift)
                if low == start:
                    weights = jnp.where(mask, weights, 0.0)
                score = weights * (dot32(value_rows[low:high], incoming) - inner)
                score = score.astype(jnp.bfloat16)
                value_sum[low:high] += dot32(weights.astype(jnp.bfloat16), back_rows[start:stop])
                key_sum[low:high] += dot32(score, query_rows[start:stop])
                part = dot32(key_low[:, low:high], score)
                grad = part if grad is None else grad + part
            grads.append(grad * score_scale)
        out, part = head_backward(
            query_ref[at, :], query_gain_ref[...], cosine, sine, jnp.concatenate(grads, axis=1)
        )
        query_back_ref[at, :] = out.astype(jnp.bfloat16)
        query_part = query_part + part
    out, part = head_backward(key_ref[...], key_gain_ref[...], cosine, sine, key_sum[...].T)
    key_back_ref[...] = out.astype(jnp.bfloat16)
    value_back_ref[...] = value_sum[...].T.astype(jnp.bfloat16)
    query_part_ref[...] = query_part
    key_part_ref[...] = part


def group_block(rows, length):
    return pl.BlockSpec((rows, length), lambda group: (group, 0))


def shared_block(rows, length):
    return pl.BlockSpec((rows, length), lambda group: (0, 0))


def attend(query, key, value, query_gain, key_gain, cosine, sine):
    width, length = cosine.shape
    groups = key.shape[0] // width
    wide = query.shape[0] // groups
    low = jnp.bfloat16
    return pl.pallas_call(
        attend_kernel,
        grid=(groups,),
        in_specs=[
            group_block(wide, length),
            group_block(width, length),
            group_block(width, length),
            shared_block(width, 1),
            shared_block(width, 1),
            shared_block(width, length),
            shared_block(width, length),
        ],
        out_specs=[
            group_block(wide, length),
            group_block(wide, length),
            group_block(width, length),
            group_block(width, length),
            group_block(8, length),
        ],
        out_shape=[
            jax.ShapeDtypeStruct(query.shape, low),
            jax.ShapeDtypeStruct(query.shape, low),
            jax.ShapeDtypeStruct(key.shape, low),
            jax.ShapeDtypeStruct(key.shape, low),
            jax.ShapeDtypeStruct((groups * 8, length), jnp.float32),
        ],
        compiler_params=pltpu.CompilerParams(vmem_limit_bytes=VMEM_LIMIT),
        cost_estimate=pl.CostEstimate(
            flops=10**10, bytes_accessed=10**7, transcendentals=query.size * length // width
        ),
        name="attend",
    )(query, key, value, query_gain, key_gain, cosine, sine)


def attend_back(query, key, query_gain, key_gain, cosine, sine, kept, mixed_back):
    mixed, query_low, key_low, value_low, total = kept
    width, length = cosine.shape
    groups = key.shape[0] // width
    wide = query.shape[0] // groups
    low = jnp.bfloat16
    return pl.pallas_call(
        attend_back_kernel,
        grid=(groups,),
        in_specs=[
            group_block(wide, length),
            group_block(width, length),
            shared_block(width, 1),
            shared_block(width, 1),
            shared_block(width, length),
            shared_block(width, length),
            group_block(wide, length),
            group_block(width, length),
            group_block(width, length),
            group_block(wide, length),
            group_block(8, length),
            group_block(wide, length),
        ],
        out_specs=[
            group_block(wide, length),
            group_block(width, length),
            group_block(width, length),
            group_block(width, 128),
            group_block(width, 128),
        ],
        out_shape=[
            jax.ShapeDtypeStruct(query.shape, low),
            jax.ShapeDtypeStruct(key.shape, low),
            jax.ShapeDtypeStruct(key.shape, low),
            jax.ShapeDtypeStruct((groups * width, 128), jnp.float32),
            jax.ShapeDtypeStruct((groups * width, 128), jnp.float32),
        ],
        scratch_shapes=[
            pltpu.VMEM((length, width), jnp.float32),
            pltpu.VMEM((length, width), jnp.float32),
        ],
        compiler_params=pltpu.CompilerParams(vmem_limit_bytes=VMEM_LIMIT),
        cost_estimate=pl.CostEstimate(
            flops=2 * 10**10, bytes_accessed=10**7, transcendentals=query.size * length // width
        ),
        name="attend_back",
    )(query, key, query_gain, key_gain, cosine, sine, query_low, key_low, value_low, mixed, total,
      mixed_back)


def cols_dot(left, right):
    return lax.dot_general(
        left, right, (((1,), (1,)), ((), ())), preferred_element_type=jnp.float32
    )


def units_kernel(sums, *refs):
    _, normed_ref, incoming_ref, gate_ref, up_ref, down_ref, *refs = refs
    hidden_ref, gate_back_ref, up_back_ref = refs[-5:-2] if sums else refs
    rows = normed_ref.shape[0]
    gate_weight, up_weight, down_weight = gate_ref[...], up_ref[...], down_ref[...]
    if sums:
        mid_ref, branch_ref = refs[-2:]

        @pl.when(pl.program_id(0) == 0)
        def _():
            if sums == 2:
                mid_ref[...], branch_ref[...] = refs[0][...], refs[1][...]
            else:
                mid_ref[...] = jnp.zeros_like(mid_ref)
                branch_ref[...] = jnp.zeros_like(branch_ref)

    for start in range(0, rows, BLOCK):
        at = slice(start, start + BLOCK)
        normed, incoming = normed_ref[at, :], incoming_ref[at, :]
        gate_act = dot32(normed, gate_weight)
        up_act = dot32(normed, up_weight)
        hidden_back = cols_dot(incoming, down_weight)
        sigmoid = 1.0 / (1.0 + jnp.exp(-gate_act))
        silu = gate_act * sigmoid
        hidden = (silu * up_act).astype(jnp.bfloat16)
        gate_in = (hidden_back * up_act * (sigmoid + silu * (1.0 - sigmoid))).astype(jnp.bfloat16)
        up_in = (hidden_back * silu).astype(jnp.bfloat16)
        hidden_ref[at, :] = hidden
        gate_back_ref[at, :] = gate_in
        up_back_ref[at, :] = up_in
        if sums:
            mid_ref[at, :] += cols_dot(gate_in, gate_weight) + cols_dot(up_in, up_weight)
            branch_ref[at, :] += dot32(hidden, down_weight)


def units_call(normed, incoming, gate_weight, up_weight, down_weight, first, count, sums, start=()):
    rows, width = normed.shape
    tile = BLOCK if count % BLOCK == 0 else BLOCK // 2
    low = jnp.bfloat16
    whole = pl.BlockSpec((rows, width), lambda at, base: (0, 0), pipeline_mode=pl.Buffered(1))
    by_unit = pl.BlockSpec((width, tile), lambda at, base: (0, base[0] + at))
    out_tile = pl.BlockSpec((rows, tile), lambda at, base: (0, at))
    out_shape = [jax.ShapeDtypeStruct((rows, count), low)] * 3
    out_specs = [out_tile] * 3
    if sums:
        out_shape = out_shape + [jax.ShapeDtypeStruct((rows, width), jnp.float32)] * 2
        out_specs = out_specs + [pl.BlockSpec((rows, width), lambda at, base: (0, 0))] * 2
    base = jnp.asarray(first // tile, jnp.int32).reshape(1)
    return pl.pallas_call(
        functools.partial(units_kernel, sums),
        grid_spec=pltpu.PrefetchScalarGridSpec(
            num_scalar_prefetch=1,
            grid=(count // tile,),
            in_specs=[
                whole,
                whole,
                by_unit,
                by_unit,
                pl.BlockSpec((tile, width), lambda at, base: (base[0] + at, 0)),
            ]
            + [whole] * len(start),
            out_specs=out_specs,
        ),
        out_shape=out_shape,
        compiler_params=pltpu.CompilerParams(vmem_limit_bytes=VMEM_LIMIT),
        cost_estimate=pl.CostEstimate(
            flops=2 * rows * width * count * (6 if sums else 3),
            bytes_accessed=10**7,
            transcendentals=rows * count,
        ),
        name="units",
    )(base, normed, incoming, gate_weight, up_weight, down_weight, *start)


def contract_cols(left_side, right_side):
    return lax.dot_general(
        left_side, right_side, (((1,), (1,)), ((), ())), preferred_element_type=jnp.float32
    )


def contract_rows(left_side, right_side):
    return lax.dot_general(
        left_side, right_side, (((0,), (0,)), ((), ())), preferred_element_type=jnp.float32
    )


def back_product(left_side, right_side):
    return lax.dot_general(
        left_side, right_side, (((0,), (1,)), ((), ())), preferred_element_type=jnp.float32
    )


def product(left_side, right_side):
    return jnp.dot(left_side, right_side, preferred_element_type=jnp.float32)


def swap(value, axis):
    return lax.ppermute(value, axis, SWAP)


def core_sum(value):
    return value + swap(value, "tensor")


def core_sum_halves(make, rows):
    half = rows // 2
    first, second = make(0, half), make(half, rows)
    return jnp.concatenate([core_sum(first), core_sum(second)], axis=0)


def tie(*values):
    return lax.optimization_barrier(values)


def line_exchange(kept, length):
    own = kept.shape[0] // length
    blocks = [kept[at * own : (at + 1) * own] for at in range(length)]
    arrived = [
        lax.ppermute(
            blocks[away], "line", [(at, (at + away) % length) for at in range(length)]
        )
        for away in range(1, length)
    ]
    return blocks[0], arrived


def line_sum(own, arrived):
    for part in arrived:
        own = own + part
    return own


def pair_sums(own, arrived):
    mine, other = own, None
    for away, part in enumerate(arrived, 1):
        if away % 2 == 0:
            mine = mine + part
        else:
            other = part if other is None else other + part
    return mine, other


def in_order(half, mine, other):
    return jnp.concatenate(
        [jnp.where(half == 0, mine, other), jnp.where(half == 0, other, mine)], axis=1
    )


class Plane:
    def __init__(self, pieces):
        self.pieces = pieces

    @staticmethod
    def rows(left, start, stop):
        quarter = left.shape[0] // 4
        return left[start * quarter : stop * quarter]

    def products(self, for_near, for_mid):
        return [
            (contract_cols if transposed else product)(
                for_near(left) if near_first else for_mid(left), right
            )
            for left, right, near_first, transposed in self.pieces
        ]

    def send(self):
        return self.products(
            lambda left: self.rows(left, 0, 2),
            lambda left: jnp.concatenate([self.rows(left, 0, 1), self.rows(left, 2, 3)], axis=0),
        )

    def go(self, out):
        return [
            swap(part, "near" if piece[2] else "mid") for part, piece in zip(out, self.pieces)
        ]

    def follow(self, got):
        parts = self.products(lambda left: self.rows(left, 2, 3), lambda left: self.rows(left, 1, 2))
        return [part + late[: part.shape[0]] for part, late in zip(parts, got)]

    def pass_on(self, out):
        return [
            swap(part, "mid" if piece[2] else "near") for part, piece in zip(out, self.pieces)
        ]

    def keep(self, got, passed):
        def own(left):
            return self.rows(left, 3, 4)

        parts = self.products(own, own)
        return jnp.concatenate(
            [
                part + early[part.shape[0] :] + late
                for part, early, late in zip(parts, got, passed)
            ],
            axis=1,
        )


class Owners:
    def __init__(self, width):
        self.length = lax.axis_size("line")
        self.width = width
        self.own = width // (4 * self.length)
        line, mid, near = (lax.axis_index(name) for name in ("line", "mid", "near"))
        place = lax.broadcasted_iota(jnp.int32, (2, 2, self.length, self.own, 1), 0)
        row = lax.broadcasted_iota(jnp.int32, place.shape, 1)
        distance = lax.broadcasted_iota(jnp.int32, place.shape, 2)
        entry = lax.broadcasted_iota(jnp.int32, place.shape, 3)
        owner_near = (place + near + 1) % 2
        owner_mid = (row + mid + 1) % 2
        owner_line = (distance + line) % self.length
        feature = ((owner_line * 2 + owner_mid) * 2 + owner_near) * self.own + entry
        self.feature = feature

    def select(self, order):
        column = lax.broadcasted_iota(jnp.int32, (1, self.width), 1)
        feature = self.feature.transpose(order + (3, 4)).reshape(self.width, 1)
        return (feature == column).astype(jnp.bfloat16)

    def plane_first(self, left):
        return contract_cols(self.select((0, 1, 2)), left).astype(jnp.bfloat16)

    def line_first(self, left):
        return contract_cols(self.select((2, 0, 1)), left).astype(jnp.bfloat16)


def line_everywhere(value):
    length = lax.axis_size("line")
    found = [value] + [
        lax.ppermute(value, "line", [(at, (at + away) % length) for at in range(length)])
        for away in range(1, length)
    ]
    return found


def in_line_order(found):
    length = len(found)
    stacked = jnp.stack(found)
    total = jnp.zeros_like(found[0])
    for at in range(length):
        away = (lax.axis_index("line") - at) % length
        total = total + lax.dynamic_index_in_dim(stacked, away, 0, keepdims=False)
    return total


def local(
    inputs,
    first_gain,
    query_weight,
    key_matrix,
    value_matrix,
    query_gain,
    key_gain,
    output_weight,
    second_gain,
    gate_weight,
    up_weight,
    down_weight,
    cotangent,
):
    row_count, model_width = inputs.shape
    head_dim = query_gain.shape[0]
    units = gate_weight.shape[1]
    cosine_table, sine_table = rope_tables(row_count, head_dim)
    owners = Owners(model_width)
    length = owners.length

    core = lax.axis_index("tensor")
    half = lax.axis_index("line") % 2
    partners = [(at, at + 1 - 2 * (at % 2)) for at in range(length)]
    core_rows = row_count // 2

    def my_rows(value):
        return lax.dynamic_slice_in_dim(value, core * core_rows, core_rows, axis=0)

    def to_partner(value):
        return lax.ppermute(value, "line", partners)

    cotangent_mine = my_rows(cotangent).astype(jnp.float32) * SHIFT
    early = core_rows // 2
    far_first = to_partner(cotangent_mine[:early])
    source = inputs.astype(jnp.float32)
    first_normed, first_pull = jax.vjp(rms_scale, source, first_gain)
    normalized_input = first_normed.astype(jnp.bfloat16)

    def project(weight):
        return lax.dot_general(
            weight,
            normalized_input,
            (((0,), (1,)), ((), ())),
            preferred_element_type=jnp.float32,
        )

    query_proj, projected_key = project(query_weight), project(key_matrix)
    gains = (query_gain[:, None], key_gain[:, None])
    kept = attend(
        query_proj, projected_key, project(value_matrix), *gains, cosine_table, sine_table
    )
    *kept, far_first, cotangent_mine = tie(*kept, far_first, cotangent_mine)
    mixed = kept[0]
    far_second = to_partner(cotangent_mine[early:])
    attention = core_sum_halves(
        lambda a, b: contract_rows(mixed[:, a:b], output_weight), row_count
    )
    middle = source + attention
    second_normed, second_pull = jax.vjp(rms_scale, middle, second_gain)
    normed_mid = second_normed.astype(jnp.bfloat16)
    hat = middle * lax.rsqrt(jnp.mean(middle * middle, axis=-1, keepdims=True) + EPSILON)
    hat, normed_mid, far_second = tie(hat, normed_mid, far_second)
    hat_far = to_partner(my_rows(hat))
    cotangent_far = jnp.concatenate([far_first, far_second], axis=0)

    weights = (gate_weight, up_weight, down_weight)

    alone = units * 2 // 9 // 256 * 256
    paired = (units - alone) // 2
    hidden_1, gate_1, up_1, *sums_1 = units_call(normed_mid, cotangent, *weights, 0, alone, 1)
    normed_left = owners.plane_first(normed_mid)
    cotangent_left = owners.plane_first(cotangent)
    up_cut = alone // 256 * 128
    plane_1 = Plane(
        [
            (cotangent_left, hidden_1, True, False),
            (normed_left, gate_1, False, False),
            (normed_left, up_1[:, :up_cut], True, False),
            (normed_left, up_1[:, up_cut:], False, False),
        ]
    )
    sent_1 = plane_1.send()
    cotangent_swapped = swap(cotangent_far, "tensor")
    sent_1, normed_mid, cotangent_swapped = tie(sent_1, normed_mid, cotangent_swapped)
    got_1 = plane_1.go(sent_1)
    hidden_2, gate_2, up_2, mid_part, branch_part = units_call(
        normed_mid, cotangent, *weights, alone, units - alone, 2, sums_1
    )
    got_1, mid_part, hat_far, cotangent_swapped = tie(got_1, mid_part, hat_far, cotangent_swapped)

    hat_swapped = swap(hat_far, "tensor")
    follow_1 = plane_1.follow(got_1)
    far_cotangent = jnp.concatenate([cotangent_far, cotangent_swapped], axis=0) * (1.0 / SHIFT)
    far_cotangent = far_cotangent.astype(jnp.bfloat16)
    follow_1, hat_far, hat_swapped, far_cotangent, mid_part = tie(
        follow_1, hat_far, hat_swapped, far_cotangent, mid_part
    )
    passed_1 = plane_1.pass_on(follow_1)
    mid_swapped = swap(mid_part, "tensor")
    far_normed = (jnp.concatenate([hat_far, hat_swapped], axis=0) * second_gain).astype(
        jnp.bfloat16
    )

    def my_half(array, start, axis):
        return lax.dynamic_slice_in_dim(array, start + half * paired, paired, axis=axis)

    far_hidden, far_gate, far_up = units_call(
        far_normed, far_cotangent, *weights, alone + half * paired, paired, 0
    )
    passed_1, far_hidden, far_gate, far_up, mid_swapped = tie(
        passed_1, far_hidden, far_gate, far_up, mid_swapped
    )
    normed_both = jnp.concatenate([normed_left, owners.plane_first(far_normed)], axis=1)
    cotangent_both = jnp.concatenate([cotangent_left, owners.plane_first(far_cotangent)], axis=1)
    hidden_both = jnp.concatenate([my_half(hidden_2, 0, 1), far_hidden], axis=0)
    gate_both = jnp.concatenate([my_half(gate_2, 0, 1), far_gate], axis=0)
    plane_2 = Plane(
        [(cotangent_both, hidden_both, True, False), (normed_both, gate_both, False, False)]
    )
    sent_2 = plane_2.send()
    sent_2, passed_1, mid_swapped = tie(sent_2, passed_1, mid_swapped)
    got_2 = plane_2.go(sent_2)
    line_1 = line_exchange(plane_1.keep(got_1, passed_1), length)
    mid_back = mid_part + mid_swapped
    middle_norm_back, second_gain_grad = second_pull(mid_back)
    middle_grad = cotangent.astype(jnp.float32) + middle_norm_back
    attention_back = middle_grad.astype(jnp.bfloat16)
    mixed_back = contract_cols(output_weight, attention_back).astype(jnp.bfloat16)
    query_back, key_back, value_back, query_part, key_part = attend_back(
        query_proj, projected_key, *gains, cosine_table, sine_table, kept, mixed_back
    )
    got_2, line_1, query_back, key_back, value_back, attention_back = tie(
        got_2, line_1, query_back, key_back, value_back, attention_back
    )
    follow_2 = plane_2.follow(got_2)
    follow_2, attention_back = tie(follow_2, attention_back)
    passed_2 = plane_2.pass_on(follow_2)
    up_both = jnp.concatenate([my_half(up_2, 0, 1), far_up], axis=0)
    plane_3 = Plane(
        [
            (normed_both, up_both, True, False),
            (owners.plane_first(attention_back), mixed, False, True),
        ]
    )
    sent_3 = plane_3.send()
    normed_part = (
        back_product(query_back, query_weight)
        + back_product(key_back, key_matrix)
        + back_product(value_back, value_matrix)
    )
    passed_2, sent_3, normed_part = tie(passed_2, sent_3, normed_part)
    got_3 = plane_3.go(sent_3)
    line_2 = line_exchange(plane_2.keep(got_2, passed_2), length)
    input_left = owners.plane_first(normalized_input)
    plane_4 = Plane(
        [
            (input_left, jnp.concatenate([key_back, value_back], axis=0), True, True),
            (input_left, query_back, False, True),
        ]
    )
    sent_4 = plane_4.send()
    got_3, line_2, sent_4, normed_part = tie(got_3, line_2, sent_4, normed_part)
    follow_3 = plane_3.follow(got_3)
    follow_3, normed_part, branch_part = tie(follow_3, normed_part, branch_part)
    passed_3 = plane_3.pass_on(follow_3)
    normed_back = core_sum(normed_part)
    source_back, first_gain_grad = first_pull(normed_back)
    input_grad = middle_grad + source_back
    passed_3, sent_4, input_grad, first_gain_grad = tie(
        passed_3, sent_4, input_grad, first_gain_grad
    )
    got_4 = plane_4.go(sent_4)
    line_3 = line_exchange(plane_3.keep(got_3, passed_3), length)
    head_gains = jnp.concatenate(
        [jnp.sum(part.reshape(-1, head_dim, 128), axis=(0, 2)) for part in (query_part, key_part)]
    )
    got_4, line_3, head_gains = tie(got_4, line_3, head_gains)
    follow_4 = plane_4.follow(got_4)
    rows = jnp.stack(
        [
            first_gain_grad,
            second_gain_grad,
            jnp.pad(core_sum(head_gains), (0, model_width - 2 * head_dim)),
        ]
    )
    rows = jnp.pad(rows, ((0, 5), (0, 0)))
    follow_4, rows = tie(follow_4, rows)
    passed_4 = plane_4.pass_on(follow_4)
    branch = core_sum(branch_part)
    result = (middle + branch).astype(jnp.bfloat16)
    rows = rows + swap(rows, "near")
    rows = rows + swap(rows, "mid")
    passed_4, rows, result = tie(passed_4, rows, result)
    line_4 = line_exchange(plane_4.keep(got_4, passed_4), length)
    rows = in_line_order(line_everywhere(rows))
    attention_shard = line_sum(*line_4)

    def split(total, count):
        return [total[:, at : at + count] for at in range(0, total.shape[1], count)]

    halves = [split(side, paired) for side in pair_sums(*line_2)]
    sides = [side[:, :paired] for side in pair_sums(*line_3)]
    down_2, gate_2, up_2 = (
        in_order(half, mine, other)
        for mine, other in zip(halves[0] + sides[:1], halves[1] + sides[1:])
    )
    first = line_sum(*line_1)
    down_1, gate_1, up_1 = first[:, :alone], first[:, alone : 2 * alone], first[:, 2 * alone :]
    down_shard, gate_shard, up_shard = (
        jnp.concatenate(pair, axis=1)
        for pair in ((down_1, down_2), (gate_1, gate_2), (up_1, up_2))
    )
    output_shard = line_sum(line_3[0][:, paired:], [part[:, paired:] for part in line_3[1]])
    key_cut = key_back.shape[0]
    pair_cut = 2 * key_cut
    index = (lax.axis_index("line") * 2 + lax.axis_index("mid")) * 2 + lax.axis_index("near")
    gains = lax.dynamic_slice(rows, (0, index * owners.own), (2, owners.own))
    return (
        result,
        input_grad,
        gains[0],
        attention_shard[:, pair_cut:],
        attention_shard[:, :key_cut],
        attention_shard[:, key_cut:pair_cut],
        rows[2, :head_dim],
        rows[2, head_dim : 2 * head_dim],
        output_shard.T,
        gains[1],
        gate_shard,
        up_shard,
        down_shard.T,
    )


def solution(mesh):
    line = mesh.shape["dp"] // 4
    shaped = Mesh(
        mesh.devices.reshape(line, 2, 2, mesh.shape["tensor"]), ("line", "mid", "near", "tensor")
    )
    dp = ("line", "mid", "near")
    placed = (
        P(dp, None),
        P(),
        P(None, "tensor"),
        P(None, "tensor"),
        P(None, "tensor"),
        P(),
        P(),
        P("tensor", None),
        P(),
        P(None, "tensor"),
        P(None, "tensor"),
        P("tensor", None),
        P(dp, None),
    )
    return jax.shard_map(
        local,
        mesh=shaped,
        in_specs=placed,
        out_specs=(
            P(dp, None),
            P(dp, None),
            P(dp),
            P(dp, "tensor"),
            P(dp, "tensor"),
            P(dp, "tensor"),
            P(),
            P(),
            P("tensor", dp),
            P(dp),
            P(dp, "tensor"),
            P(dp, "tensor"),
            P("tensor", dp),
        ),
        check_vma=False,
    )
```

time: 1150 us -> 463 us (0.40)
  waiting for transfers between devices: 791 us -> 104 us
  Pallas kernels: 0 us -> 102 us
  matrix products: 178 us -> 94.3 us
  blocking collectives: 82.1 us -> 0 us
  starting transfers between devices: 0.82 us -> 67 us
  local copies, waits for them, and re-layouts: 16.2 us -> 30.2 us
  between operations: 16.1 us -> 2.27 us
    reduce_scatter x7 -> x0, waiting for transfers between devices: 740 us -> none  [the longest x1 177 us: local(): lax.psum_scatter(up_grad, 'dp', scatter_dimension=0, tiled=True)]
    ppermute x0 -> x48, waiting for transfers between devices: none -> 104 us  [the longest x12 61.8 us: line_exchange(): lax.ppermute(blocks[away], 'line', [(at, (at + away) % length) for at in...]
    pallas_call x0 -> x5, Pallas kernels: none -> 102 us  [the longest x3 70.2 us: units_call(): pl.pallas_call(functools.partial(units_kernel, sums), grid_spec=pltpu.Pre...]
    ppermute x0 -> x48, starting transfers between devices: none -> 67 us  [the longest x12 25.4 us: line_exchange(): lax.ppermute(blocks[away], 'line', [(at, (at + away) % length) for at in...]
    psum x3 -> x0, waiting for transfers between devices: 51.1 us -> none  [the longest x1 31.2 us: local(): lax.psum(jnp.dot(mixed, output_weight, preferred_element_type=jnp.float32...]
    dot_general x7 -> x2, matrix products: 47.5 us -> 5.14 us  [contract_rows(): lax.dot_general(left_side, right_side, (((0,), (0,)), ((), ())), preferre...]
    unnamed x1 -> x0, blocking collectives: 41.3 us -> none
    psum x1 -> x0, blocking collectives: 40.8 us -> none  [local(): lax.psum((query_gain_part, key_gain_part), ('dp', 'tensor'))]
  transfers between devices with their start and end apart: 10 -> 48, of which waited for: 8 -> 15; matrix products, arithmetic and copies ran while one was open for 6% -> 30% of each run, Pallas kernels for 0% -> 22%
where the time goes in v1:
time: 463 us; the launch traced here: 459 us
  waiting for transfers between devices  104 us (22%)
  Pallas kernels  102 us (22%)
  matrix products  94.3 us (20%)
  starting transfers between devices  67 us (14%)
  other arithmetic  58.4 us (13%)
  local copies, waits for them, and re-layouts  30.2 us (7%)
    pallas_call x3, Pallas kernels, units_call(): pl.pallas_call(functools.partial(units_kernel, sums), grid_spec=pltpu.Pre...  70.2 us
    ppermute x12, waiting for transfers between devices, line_exchange(): lax.ppermute(blocks[away], 'line', [(at, (at + away) % length) for at in...  61.8 us
    dot_general x21, matrix products, product(): return jnp.dot(left_side, right_side, preferred_element_type=jnp.float32)  47.4 us
    ppermute x30, waiting for transfers between devices, swap(): return lax.ppermute(value, axis, SWAP)  30.4 us
    dot_general x16, matrix products, contract_cols(): lax.dot_general(left_side, right_side, (((1,), (1,)), ((), ())), preferre...  30.3 us
    ppermute x12, starting transfers between devices, line_exchange(): lax.ppermute(blocks[away], 'line', [(at, (at + away) % length) for at in...  25.4 us
    ppermute x30, starting transfers between devices, swap(): return lax.ppermute(value, axis, SWAP)  24.2 us
    pallas_call x1, Pallas kernels, attend_back(): pl.pallas_call(attend_back_kernel, grid=(groups,), in_specs=[group_block(...  20.6 us
  transfers between devices with their start and end apart: 48, of which 15 were waited for; matrix products, arithmetic and copies ran while one was open for 30% of the time, Pallas kernels for 22%

profile of v1, /device:TPU:0, one launch (start us, length us, event | category | flops | bytes accessed | tf_op | source)
XLA Modules:
  0.0 458.7 jit_solution(3096477556987850942)
XLA Ops:
  4.7 3.0 collective-permute-start
  8.8 2.8 convolution_bitcast_fusion.query_ref
  11.6 1.9 convolution_bitcast_fusion.2.key_ref
  13.5 1.9 convolution_bitcast_fusion.1.value_ref
  16.9 1.9 fusion.126
  18.8 11.3 %attend.1 = (bf16[512,1024]{1,0:T(8,128)(2,1)}, bf16[512,1024]{1,0:T(8,128)(2,1)}, bf16[256,1024]{1,0:T(8,128)(2,1)}, bf16[256,1024]{1,0:T(8,128)(2,1)}, f32[32,1024]{1,0:T(8,128)}) custom-call(f32[512,1024]{1,0:T(8,128)} %convolution_bitcast_fusion.query_ref, f32[256,1024]{1,0:T(8,128)} %convolution_bitcast_fusion.2.key_ref, ...), custom_call_target="tpu_custom_call" | custom-call | flops 10000000000 | bytes 10000000 | tf_op jit(solution)/shard_map/attend/pallas_call | solution.py:181
  31.2 3.1 fusion.87
  34.3 2.0 fusion.89
  38.9 1.8 collective-permute-start.3
  40.7 3.9 fusion.33
  44.6 2.8 add.389
  47.4 3.5 add.388
  53.0 11.0 %collective-permute-done.3 = f32[256,1024]{1,0:T(8,128)S(1)} collective-permute-done((f32[256,1024]{1,0:T(8,128)S(1)}, f32[256,1024]{1,0:T(8,128)S(1)}, u32[]{:S(2)}, u32[]{:S(2)}) %collective-permute-start.3) | collective-permute-done | bytes 1048608 | tf_op jit(solution)/shard_map/ppermute | solution.py:548
  64.0 2.4 fusion.34
  66.4 3.5 pad_maximum_fusion.3
  74.2 15.2 %units.3 = (bf16[1024,512]{1,0:T(8,128)(2,1)}, bf16[1024,512]{1,0:T(8,128)(2,1)}, bf16[1024,512]{1,0:T(8,128)(2,1)}, f32[1024,1024]{1,0:T(8,128)}, f32[1024,1024]{1,0:T(8,128)}) custom-call(s32[1]{0:T(128)} %constant.121.clone.1.refs_0_, bf16[1024,1024]{1,0:T(8,128)(2,1)} %copy-done.43, bf16[1024,1024]{1,0:T(8,128)(2,1)} %refs_2_.3, ...), custom_call_target="tpu_custom_call" | custom-call | flops 6442450944 | bytes 10000000 | tf_op jit(solution)/shard_map/units/pallas_call | solution.py:319
  89.4 2.6 fusion.78
  92.1 2.3 fusion.66
  102.4 38.4 %units.4 = (bf16[1024,1792]{1,0:T(8,128)(2,1)}, bf16[1024,1792]{1,0:T(8,128)(2,1)}, bf16[1024,1792]{1,0:T(8,128)(2,1)}, f32[1024,1024]{1,0:T(8,128)}, f32[1024,1024]{1,0:T(8,128)}) custom-call(s32[1]{0:T(128)} %constant.126.clone.1.refs_0_, bf16[1024,1024]{1,0:T(8,128)(2,1)} %copy-done.43, bf16[1024,1024]{1,0:T(8,128)(2,1)} %refs_2_.3, ...), custom_call_target="tpu_custom_call" | custom-call | flops 22548578304 | bytes 10000000 | tf_op jit(solution)/shard_map/units/pallas_call | solution.py:319
  140.9 4.3 fusion.8.refs_2_
  146.3 2.0 slice_add_fusion.2
  148.3 2.5 slice_add_fusion.1
  150.8 2.3 slice_add_fusion
  153.3 2.5 fusion.32
  159.6 2.1 constant_dynamic-slice_fusion.2
  165.8 4.1 fusion.9.refs_1_
  169.9 3.9 fusion.35
  173.8 16.6 %units.5 = (bf16[1024,896]{1,0:T(8,128)(2,1)}, bf16[1024,896]{1,0:T(8,128)(2,1)}, bf16[1024,896]{1,0:T(8,128)(2,1)}) custom-call(s32[1]{0:T(128)} %bitcast.5.refs_0_, bf16[1024,1024]{1,0:T(8,128)(2,1)} %fusion.9.refs_1_, bf16[1024,1024]{1,0:T(8,128)(2,1)} %fusion.8.refs_2_, bf16[1024,2304]{1,0:T(8,128)(2,1)} %refs_3_.5, bf16[1024,2304]{1,0:T(8,128)(2,1)} %refs_4_.5, ...), custom_call_target="tpu_custom_call" | custom-call | flops 5637144576 | bytes 10000000 | tf_op jit(solution)/shard_map/units/pallas_call | solution.py:319
  190.4 4.1 fusion.36
  198.9 3.6 fusion.17
  202.5 3.6 fusion.22
  212.4 1.8 add_add_fusion.4
  215.9 2.6 collective-permute-start.19
  218.4 2.5 collective-permute-start.20
  220.9 5.0 %multiply_reduce_fusion = (f32[1024]{0:T(1024)}, f32[1024]{0:T(1024)S(1)}) fusion(f32[1024,1024]{1,0:T(8,128)S(1)} %copy-done.9, f32[1024,1024]{1,0:T(8,128)} %get-tuple-element.174, f32[1024,1024]{1,0:T(8,128)} %collective-permute-done.15, f32[1024]{0:T(1024)S(1)} %copy-done.83, f32[512,1024]{1,0:T(8,128)S(1)} %copy-done.3, f32[512,1024]{1,0:T(8,128)S(1)} %copy-done.6, ...), kind=kLoop, calls=%fused_computation.32 | loop fusion | flops 9435136 | bytes 18886656 | tf_op jit(solution)/shard_map/transpose(jvp())/reduce_sum | solution.py:20
  226.0 5.9 %fusion.162 = (bf16[1024,1024]{1,0:T(8,128)(2,1)S(1)}, f32[1024,1024]{1,0:T(8,128)}) fusion(f32[1024]{0:T(1024)S(1)} %multiply_multiply_fusion.1, f32[512,1024]{1,0:T(8,128)S(1)} %copy-done.3, f32[512,1024]{1,0:T(8,128)S(1)} %copy-done.6, bf16[1024,1024]{1,0:T(8,128)(2,1)S(1)} %copy-done.1, f32[1024]{0:T(1024)S(1)} %fusion.138, f32[1024]{0:T(1024)S(1)} %copy-done.83, ...), kind=kLoop, calls=%fused_computation.272 | loop fusion | flops 12582912 | bytes 23080960 | tf_op jit(solution)/shard_map/convert_element_type | solution.py:645
  233.2 2.3 fusion.38.back_ref
  235.5 20.6 %attend_back.1 = (bf16[512,1024]{1,0:T(8,128)(2,1)}, bf16[256,1024]{1,0:T(8,128)(2,1)}, bf16[256,1024]{1,0:T(8,128)(2,1)}, f32[256,128]{1,0:T(8,128)}, f32[256,128]{1,0:T(8,128)}) custom-call(f32[512,1024]{1,0:T(8,128)} %convolution_bitcast_fusion.query_ref, f32[256,1024]{1,0:T(8,128)} %convolution_bitcast_fusion.2.key_ref, f32[64,1]{1,0:T(8,128)} %copy.40.query_gain_ref, ...), custom_call_target="tpu_custom_call" | custom-call | flops 20000000000 | bytes 10000000 | tf_op jit(solution)/shard_map/attend_back/pallas_call | solution.py:221
  256.2 5.2 %fusion.20 = f32[512,896]{1,0:T(8,128)S(1)} fusion(bf16[1024,1024]{1,0:T(8,128)(2,1)} %copy-done.11, bf16[1024,1024]{1,0:T(8,128)(2,1)} %copy-done.36, bf16[1024,896]{1,0:T(8,128)(2,1)} %get-tuple-element.200, bf16[1024,896]{1,0:T(8,128)(2,1)} %constant_dynamic-slice_fusion.1), kind=kOutput, calls=%fused_computation.59 | convolution fusion | flops 1890582528 | bytes 9699328 | tf_op jit(solution)/shard_map/dot_general | solution.py:364
  261.5 2.6 fusion.54
  265.0 2.6 fusion.49
  268.7 2.4 fusion.37
  271.2 1.9 copy-done.27
  277.2 2.8 add_add_fusion.2
  280.0 7.7 %collective-permute-done.21 = f32[256,896]{1,0:T(8,128)S(1)} collective-permute-done((f32[256,896]{1,0:T(8,128)S(1)}, f32[256,896]{1,0:T(8,128)S(1)}, u32[]{:S(2)}, u32[]{:S(2)}) %collective-permute-start.21) | collective-permute-done | bytes 917536 | tf_op jit(solution)/shard_map/ppermute | solution.py:368
  292.5 2.5 fusion.56
  295.0 2.7 fusion.51
  299.3 3.1 collective-permute-start.27
  305.2 8.7 %collective-permute-done.25 = f32[64,1792]{1,0:T(8,128)S(1)} collective-permute-done((f32[64,1792]{1,0:T(8,128)S(1)}, f32[64,1792]{1,0:T(8,128)S(1)}, u32[]{:S(2)}, u32[]{:S(2)}) %collective-permute-start.25) | collective-permute-done | bytes 458784 | tf_op jit(solution)/shard_map/ppermute | solution.py:389
  313.9 14.0 %collective-permute-done.26 = f32[64,1792]{1,0:T(8,128)S(1)} collective-permute-done((f32[64,1792]{1,0:T(8,128)S(1)}, f32[64,1792]{1,0:T(8,128)S(1)}, u32[]{:S(2)}, u32[]{:S(2)}) %collective-permute-start.26) | collective-permute-done | bytes 458784 | tf_op jit(solution)/shard_map/ppermute | solution.py:389
  328.8 2.2 fusion.44
  339.8 6.0 %collective-permute-done.41 = f32[1024,1024]{1,0:T(8,128)} collective-permute-done((f32[1024,1024]{1,0:T(8,128)}, f32[1024,1024]{1,0:T(8,128)}, u32[]{:S(2)}, u32[]{:S(2)}) %collective-permute-start.41) | collective-permute-done | bytes 4194336 | tf_op jit(solution)/shard_map/ppermute | solution.py:368
  345.8 8.4 %fusion.3 = (f32[1024]{0:T(1024)S(1)}, f32[1024]{0:T(1024)S(1)}, bf16[1024,1024]{1,0:T(8,128)(2,1)}) fusion(bf16[1024,1024]{1,0:T(8,128)(2,1)S(1)} %copy-done.1, f32[1024]{0:T(1024)S(1)} %fusion.137, f32[1024,1024]{1,0:T(8,128)} %add_add_fusion.2, f32[1024,1024]{1,0:T(8,128)} %collective-permute-done.30, f32[1024]{0:T(1024)S(1)} %copy-done.88, ...), kind=kLoop, calls=%fused_computation.22 | loop fusion | flops 13629440 | bytes 25182208 | tf_op jit(solution)/shard_map/transpose(jvp())/reduce_sum | solution.py:20
  354.3 5.6 %fusion.5 = f32[1024,1024]{1,0:T(8,128)} fusion(f32[1024,1024]{1,0:T(8,128)S(1)} %copy-done.10, bf16[1024,1024]{1,0:T(8,128)(2,1)S(1)} %copy-done.1, f32[1024]{0:T(1024)S(1)} %multiply_multiply_fusion, f32[1024]{0:T(1024)S(1)} %copy-done.88, f32[1024]{0:T(1024)S(1)} %fusion.137, f32[1024,1024]{1,0:T(8,128)} %add_add_fusion.2, ...), kind=kLoop, calls=%fused_computation.24 | loop fusion | flops 8388608 | bytes 18886656 | tf_op jit(solution)/shard_map/add | solution.py:686
  365.1 9.2 %collective-permute-start.33 = (f32[64,1408]{1,0:T(8,128)S(1)}, f32[64,1408]{1,0:T(8,128)S(1)}, u32[]{:S(2)}, u32[]{:S(2)}) collective-permute-start(f32[64,1408]{1,0:T(8,128)S(1)} %get-tuple-element.283), channel_id=1, source_target_pairs={{0,8},{8,16},{16,24},{24,0},{1,9},{9,17},{17,25},{25,1},{2,10},{10... | collective-permute-start | bytes 1081352 | tf_op jit(solution)/shard_map/ppermute | solution.py:389
  374.7 2.1 collective-permute-start.35
  378.5 5.0 %collective-permute-done.33 = f32[64,1408]{1,0:T(8,128)S(1)} collective-permute-done((f32[64,1408]{1,0:T(8,128)S(1)}, f32[64,1408]{1,0:T(8,128)S(1)}, u32[]{:S(2)}, u32[]{:S(2)}) %collective-permute-start.33) | collective-permute-done | bytes 360480 | tf_op jit(solution)/shard_map/ppermute | solution.py:389
  383.5 14.6 %collective-permute-done.34 = f32[64,1408]{1,0:T(8,128)S(1)} collective-permute-done((f32[64,1408]{1,0:T(8,128)S(1)}, f32[64,1408]{1,0:T(8,128)S(1)}, u32[]{:S(2)}, u32[]{:S(2)}) %collective-permute-start.34) | collective-permute-done | bytes 360480 | tf_op jit(solution)/shard_map/ppermute | solution.py:389
  404.5 11.6 %collective-permute-done.39 = f32[8,1024]{1,0:T(8,128)S(1)} collective-permute-done((f32[8,1024]{1,0:T(8,128)S(1)}, f32[8,1024]{1,0:T(8,128)S(1)}, u32[]{:S(2)}, u32[]{:S(2)}) %collective-permute-start.39) | collective-permute-done | bytes 32800 | tf_op jit(solution)/shard_map/ppermute | solution.py:368
  417.6 2.4 collective-permute-done.40
  420.0 10.2 %collective-permute-start.44 = (f32[8,1024]{1,0:T(8,128)S(1)}, f32[8,1024]{1,0:T(8,128)S(1)}, u32[]{:S(2)}, u32[]{:S(2)}) collective-permute-start(f32[8,1024]{1,0:T(8,128)S(1)} %add.429), channel_id=1, source_target_pairs={{0,24},{8,0},{16,8},{24,16},{1,25},{9,1},{17,9},{25,17},{2,26},{10... | collective-permute-start | bytes 98312 | tf_op jit(solution)/shard_map/ppermute | solution.py:501
  431.9 3.2 collective-permute-start.47
  437.6 4.3 collective-permute-done.47
  441.9 15.2 %collective-permute-done.46 = f32[64,1024]{1,0:T(8,128)S(1)} collective-permute-done((f32[64,1024]{1,0:T(8,128)S(1)}, f32[64,1024]{1,0:T(8,128)S(1)}, u32[]{:S(2)}, u32[]{:S(2)}) %collective-permute-start.46) | collective-permute-done | bytes 262176 | tf_op jit(solution)/shard_map/ppermute | solution.py:389
  (377 shorter events, 92.7 us)
Async XLA Ops:
  0.6 30.5 %copy-start = (bf16[512,1024]{1,0:T(8,128)(2,1)S(1)}, bf16[512,1024]{1,0:T(8,128)(2,1)}, u32[]{:S(2)}) copy-start(bf16[512,1024]{1,0:T(8,128)(2,1)} %param.20) | copy-start | bytes 3145732
  4.7 26.5 %collective-permute-start = (f32[256,1024]{1,0:T(8,128)}, f32[256,1024]{1,0:T(8,128)}, u32[]{:S(2)}, u32[]{:S(2)}) collective-permute-start(f32[256,1024]{1,0:T(8,128)} %slice.362), channel_id=1, source_target_pairs={{0,8},{8,0},{16,24},{24,16},{1,9},{9,1},{17,25},{25,17},{2,10},{10... | collective-permute-start | bytes 3145736 | tf_op jit(solution)/shard_map/ppermute | solution.py:548
  34.3 10.4 %collective-permute-start.2 = (f32[512,1024]{1,0:T(8,128)}, f32[512,1024]{1,0:T(8,128)}, u32[]{:S(2)}, u32[]{:S(2)}) collective-permute-start(f32[512,1024]{1,0:T(8,128)} %fusion.87), channel_id=1, source_target_pairs={{0,1},{1,0},{2,3},{3,2},{4,5},{5,4},{6,7},{7,6},{8,9},{9,8},{10,11... | collective-permute-start | bytes 6291464 | tf_op jit(solution)/shard_map/ppermute | solution.py:368
  36.3 11.1 %collective-permute-start.1 = (f32[512,1024]{1,0:T(8,128)}, f32[512,1024]{1,0:T(8,128)}, u32[]{:S(2)}, u32[]{:S(2)}) collective-permute-start(f32[512,1024]{1,0:T(8,128)} %fusion.89), channel_id=1, source_target_pairs={{0,1},{1,0},{2,3},{3,2},{4,5},{5,4},{6,7},{7,6},{8,9},{9,8},{10,11... | collective-permute-start | bytes 6291464 | tf_op jit(solution)/shard_map/ppermute | solution.py:368
  37.4 153.0 %copy-start.89 = (s32[1024]{0:T(1024)}, s32[1024]{0:T(1024)S(1)}, u32[]{:S(2)}) copy-start(s32[1024]{0:T(1024)S(1)} %fusion.134) | copy-start | bytes 12292
  38.9 25.1 %collective-permute-start.3 = (f32[256,1024]{1,0:T(8,128)S(1)}, f32[256,1024]{1,0:T(8,128)S(1)}, u32[]{:S(2)}, u32[]{:S(2)}) collective-permute-start(f32[256,1024]{1,0:T(8,128)S(1)} %slice.278), channel_id=1, source_target_pairs={{0,8},{8,0},{16,24},{24,16},{1,9},{9,1},{17,25},{25,17},{2,10},{10... | collective-permute-start | bytes 3145736 | tf_op jit(solution)/shard_map/ppermute | solution.py:548
  52.9 13.5 %copy-start.43 = (bf16[1024,1024]{1,0:T(8,128)(2,1)}, bf16[1024,1024]{1,0:T(8,128)(2,1)S(1)}, u32[]{:S(2)}) copy-start(bf16[1024,1024]{1,0:T(8,128)(2,1)S(1)} %get-tuple-element.150.refs_1_) | copy-start | bytes 6291460
  53.0 17.0 %copy-start.8 = (f32[1024,1024]{1,0:T(8,128)}, f32[1024,1024]{1,0:T(8,128)S(1)}, u32[]{:S(2)}) copy-start(f32[1024,1024]{1,0:T(8,128)S(1)} %get-tuple-element.154) | copy-start | bytes 12582916
  70.0 28.4 %collective-permute-start.4 = (f32[512,1024]{1,0:T(8,128)}, f32[512,1024]{1,0:T(8,128)}, u32[]{:S(2)}, u32[]{:S(2)}) collective-permute-start(f32[512,1024]{1,0:T(8,128)} %pad_maximum_fusion.3), channel_id=1, source_target_pairs={{0,1},{1,0},{2,3},{3,2},{4,5},{5,4},{6,7},{7,6},{8,9},{9,8},{10,11... | collective-permute-start | bytes 6291464 | tf_op jit(solution)/shard_map/ppermute | solution.py:368
  71.6 69.2 %collective-permute-start.9 = (f32[512,1024]{1,0:T(8,128)}, f32[512,1024]{1,0:T(8,128)}, u32[]{:S(2)}, u32[]{:S(2)}) collective-permute-start(f32[512,1024]{1,0:T(8,128)} %constant_dynamic-slice_fusion.4), channel_id=1, source_target_pairs={{0,8},{8,0},{16,24},{24,16},{1,9},{9,1},{17,25},{25,17},{2,10},{10... | collective-permute-start | bytes 6291464 | tf_op jit(solution)/shard_map/ppermute | solution.py:548
  98.4 42.5 %collective-permute-start.5 = (f32[512,512]{1,0:T(8,128)}, f32[512,512]{1,0:T(8,128)}, u32[]{:S(2)}, u32[]{:S(2)}) collective-permute-start(f32[512,512]{1,0:T(8,128)} %fusion.68), channel_id=1, source_target_pairs={{0,2},{2,0},{1,3},{3,1},{4,6},{6,4},{5,7},{7,5},{8,10},{10,8},{9,1... | collective-permute-start | bytes 3145736 | tf_op jit(solution)/shard_map/ppermute | solution.py:368
  99.8 41.0 %collective-permute-start.6 = (f32[512,512]{1,0:T(8,128)}, f32[512,512]{1,0:T(8,128)}, u32[]{:S(2)}, u32[]{:S(2)}) collective-permute-start(f32[512,512]{1,0:T(8,128)} %fusion.79), channel_id=1, source_target_pairs={{0,4},{4,0},{1,5},{5,1},{2,6},{6,2},{3,7},{7,3},{8,12},{12,8},{9,1... | collective-permute-start | bytes 3145736 | tf_op jit(solution)/shard_map/ppermute | solution.py:368
  101.4 39.4 %collective-permute-start.7 = (f32[512,256]{1,0:T(8,128)}, f32[512,256]{1,0:T(8,128)S(1)}, u32[]{:S(2)}, u32[]{:S(2)}) collective-permute-start(f32[512,256]{1,0:T(8,128)} %fusion.66), channel_id=1, source_target_pairs={{0,2},{2,0},{1,3},{3,1},{4,6},{6,4},{5,7},{7,5},{8,10},{10,8},{9,1... | collective-permute-start | bytes 1572872 | tf_op jit(solution)/shard_map/ppermute | solution.py:368
  101.9 38.9 %collective-permute-start.8 = (f32[512,256]{1,0:T(8,128)}, f32[512,256]{1,0:T(8,128)}, u32[]{:S(2)}, u32[]{:S(2)}) collective-permute-start(f32[512,256]{1,0:T(8,128)} %fusion.78), channel_id=1, source_target_pairs={{0,4},{4,0},{1,5},{5,1},{2,6},{6,2},{3,7},{7,3},{8,12},{12,8},{9,1... | collective-permute-start | bytes 1572872 | tf_op jit(solution)/shard_map/ppermute | solution.py:368
  140.9 12.2 %collective-permute-start.10 = (f32[512,1024]{1,0:T(8,128)}, f32[512,1024]{1,0:T(8,128)}, u32[]{:S(2)}, u32[]{:S(2)}) collective-permute-start(f32[512,1024]{1,0:T(8,128)} %collective-permute-done.9), channel_id=1, source_target_pairs={{0,1},{1,0},{2,3},{3,2},{4,5},{5,4},{6,7},{7,6},{8,9},{9,8},{10,11... | collective-permute-start | bytes 6291464 | tf_op jit(solution)/shard_map/ppermute | solution.py:368
  153.0 43.2 %collective-permute-start.15 = (f32[1024,1024]{1,0:T(8,128)}, f32[1024,1024]{1,0:T(8,128)}, u32[]{:S(2)}, u32[]{:S(2)}) collective-permute-start(f32[1024,1024]{1,0:T(8,128)} %get-tuple-element.174), channel_id=1, source_target_pairs={{0,1},{1,0},{2,3},{3,2},{4,5},{5,4},{6,7},{7,6},{8,9},{9,8},{10,11... | collective-permute-start | bytes 12582920 | tf_op jit(solution)/shard_map/ppermute | solution.py:368
  161.7 34.5 %collective-permute-start.11 = (f32[256,512]{1,0:T(8,128)}, f32[256,512]{1,0:T(8,128)}, u32[]{:S(2)}, u32[]{:S(2)}) collective-permute-start(f32[256,512]{1,0:T(8,128)} %slice_add_fusion.1), channel_id=1, source_target_pairs={{0,4},{4,0},{1,5},{5,1},{2,6},{6,2},{3,7},{7,3},{8,12},{12,8},{9,1... | collective-permute-start | bytes 1572872 | tf_op jit(solution)/shard_map/ppermute | solution.py:368
  163.3 33.0 %collective-permute-start.12 = (f32[256,512]{1,0:T(8,128)S(1)}, f32[256,512]{1,0:T(8,128)}, u32[]{:S(2)}, u32[]{:S(2)}) collective-permute-start(f32[256,512]{1,0:T(8,128)S(1)} %copy-done.66), channel_id=1, source_target_pairs={{0,2},{2,0},{1,3},{3,1},{4,6},{6,4},{5,7},{7,5},{8,10},{10,8},{9,1... | collective-permute-start | bytes 1572872 | tf_op jit(solution)/shard_map/ppermute | solution.py:368
  164.7 31.5 %collective-permute-start.13 = (f32[256,256]{1,0:T(8,128)}, f32[256,256]{1,0:T(8,128)S(1)}, u32[]{:S(2)}, u32[]{:S(2)}) collective-permute-start(f32[256,256]{1,0:T(8,128)} %slice_add_fusion.3), channel_id=1, source_target_pairs={{0,4},{4,0},{1,5},{5,1},{2,6},{6,2},{3,7},{7,3},{8,12},{12,8},{9,1... | collective-permute-start | bytes 786440 | tf_op jit(solution)/shard_map/ppermute | solution.py:368
  165.3 31.0 %collective-permute-start.14 = (f32[256,256]{1,0:T(8,128)}, f32[256,256]{1,0:T(8,128)}, u32[]{:S(2)}, u32[]{:S(2)}) collective-permute-start(f32[256,256]{1,0:T(8,128)} %slice_add_fusion.2), channel_id=1, source_target_pairs={{0,2},{2,0},{1,3},{3,1},{4,6},{6,4},{5,7},{7,5},{8,10},{10,8},{9,1... | collective-permute-start | bytes 786440 | tf_op jit(solution)/shard_map/ppermute | solution.py:368
  206.1 55.3 %collective-permute-start.16 = (f32[512,896]{1,0:T(8,128)}, f32[512,896]{1,0:T(8,128)}, u32[]{:S(2)}, u32[]{:S(2)}) collective-permute-start(f32[512,896]{1,0:T(8,128)} %fusion.17), channel_id=1, source_target_pairs={{0,2},{2,0},{1,3},{3,1},{4,6},{6,4},{5,7},{7,5},{8,10},{10,8},{9,1... | collective-permute-start | bytes 5505032 | tf_op jit(solution)/shard_map/ppermute | solution.py:368
  207.6 53.8 %collective-permute-start.17 = (f32[512,896]{1,0:T(8,128)}, f32[512,896]{1,0:T(8,128)}, u32[]{:S(2)}, u32[]{:S(2)}) collective-permute-start(f32[512,896]{1,0:T(8,128)} %fusion.22), channel_id=1, source_target_pairs={{0,4},{4,0},{1,5},{5,1},{2,6},{6,2},{3,7},{7,3},{8,12},{12,8},{9,1... | collective-permute-start | bytes 5505032 | tf_op jit(solution)/shard_map/ppermute | solution.py:368
  215.4 45.9 %collective-permute-start.18 = (f32[64,1536]{1,0:T(8,128)}, f32[64,1536]{1,0:T(8,128)}, u32[]{:S(2)}, u32[]{:S(2)}) collective-permute-start(f32[64,1536]{1,0:T(8,128)} %get-tuple-element.277), channel_id=1, source_target_pairs={{0,8},{8,16},{16,24},{24,0},{1,9},{9,17},{17,25},{25,1},{2,10},{10... | collective-permute-start | bytes 1179656 | tf_op jit(solution)/shard_map/ppermute | solution.py:389
  215.9 45.5 %collective-permute-start.19 = (f32[64,1536]{1,0:T(8,128)}, f32[64,1536]{1,0:T(8,128)}, u32[]{:S(2)}, u32[]{:S(2)}) collective-permute-start(f32[64,1536]{1,0:T(8,128)} %get-tuple-element.276), channel_id=1, source_target_pairs={{0,16},{8,24},{16,0},{24,8},{1,17},{9,25},{17,1},{25,9},{2,18},{10... | collective-permute-start | bytes 1179656 | tf_op jit(solution)/shard_map/ppermute | solution.py:389
  218.4 42.9 %collective-permute-start.20 = (f32[64,1536]{1,0:T(8,128)S(1)}, f32[64,1536]{1,0:T(8,128)}, u32[]{:S(2)}, u32[]{:S(2)}) collective-permute-start(f32[64,1536]{1,0:T(8,128)S(1)} %get-tuple-element.275), channel_id=1, source_target_pairs={{0,24},{8,0},{16,8},{24,16},{1,25},{9,1},{17,9},{25,17},{2,26},{10... | collective-permute-start | bytes 1179656 | tf_op jit(solution)/shard_map/ppermute | solution.py:389
  267.6 20.1 %collective-permute-start.21 = (f32[256,896]{1,0:T(8,128)S(1)}, f32[256,896]{1,0:T(8,128)S(1)}, u32[]{:S(2)}, u32[]{:S(2)}) collective-permute-start(f32[256,896]{1,0:T(8,128)S(1)} %fusion.54), channel_id=1, source_target_pairs={{0,4},{4,0},{1,5},{5,1},{2,6},{6,2},{3,7},{7,3},{8,12},{12,8},{9,1... | collective-permute-start | bytes 2752520 | tf_op jit(solution)/shard_map/ppermute | solution.py:368
  268.2 20.4 %collective-permute-start.22 = (f32[256,896]{1,0:T(8,128)S(1)}, f32[256,896]{1,0:T(8,128)S(1)}, u32[]{:S(2)}, u32[]{:S(2)}) collective-permute-start(f32[256,896]{1,0:T(8,128)S(1)} %fusion.49), channel_id=1, source_target_pairs={{0,2},{2,0},{1,3},{3,1},{4,6},{6,4},{5,7},{7,5},{8,10},{10,8},{9,1... | collective-permute-start | bytes 2752520 | tf_op jit(solution)/shard_map/ppermute | solution.py:368
  271.1 59.9 %copy-start.42 = (bf16[1024,1024]{1,0:T(8,128)(2,1)}, bf16[1024,1024]{1,0:T(8,128)(2,1)S(1)}, u32[]{:S(2)}) copy-start(bf16[1024,1024]{1,0:T(8,128)(2,1)S(1)} %fusion.37) | copy-start | bytes 6291460
  277.2 12.0 %copy-start.70 = (bf16[256,1024]{1,0:T(8,128)(2,1)S(1)}, bf16[256,1024]{1,0:T(8,128)(2,1)}, u32[]{:S(2)}) copy-start(bf16[256,1024]{1,0:T(8,128)(2,1)} %get-tuple-element.265) | copy-start | bytes 1572868
  277.2 12.0 %copy-start.71 = (bf16[256,1024]{1,0:T(8,128)(2,1)S(1)}, bf16[256,1024]{1,0:T(8,128)(2,1)}, u32[]{:S(2)}) copy-start(bf16[256,1024]{1,0:T(8,128)(2,1)} %get-tuple-element.266) | copy-start | bytes 1572868
  288.6 39.2 %collective-permute-start.23 = (f32[512,896]{1,0:T(8,128)S(1)}, f32[512,896]{1,0:T(8,128)S(1)}, u32[]{:S(2)}, u32[]{:S(2)}) collective-permute-start(f32[512,896]{1,0:T(8,128)S(1)} %fusion.20), channel_id=1, source_target_pairs={{0,2},{2,0},{1,3},{3,1},{4,6},{6,4},{5,7},{7,5},{8,10},{10,8},{9,1... | collective-permute-start | bytes 5505032 | tf_op jit(solution)/shard_map/ppermute | solution.py:368
  290.9 37.0 %collective-permute-start.24 = (f32[512,512]{1,0:T(8,128)S(1)}, f32[512,512]{1,0:T(8,128)S(1)}, u32[]{:S(2)}, u32[]{:S(2)}) collective-permute-start(f32[512,512]{1,0:T(8,128)S(1)} %fusion.70), channel_id=1, source_target_pairs={{0,4},{4,0},{1,5},{5,1},{2,6},{6,2},{3,7},{7,3},{8,12},{12,8},{9,1... | collective-permute-start | bytes 3145736 | tf_op jit(solution)/shard_map/ppermute | solution.py:368
  298.6 15.3 %collective-permute-start.25 = (f32[64,1792]{1,0:T(8,128)S(1)}, f32[64,1792]{1,0:T(8,128)S(1)}, u32[]{:S(2)}, u32[]{:S(2)}) collective-permute-start(f32[64,1792]{1,0:T(8,128)S(1)} %get-tuple-element.273), channel_id=1, source_target_pairs={{0,8},{8,16},{16,24},{24,0},{1,9},{9,17},{17,25},{25,1},{2,10},{10... | collective-permute-start | bytes 1376264 | tf_op jit(solution)/shard_map/ppermute | solution.py:389
  298.6 29.3 %collective-permute-start.26 = (f32[64,1792]{1,0:T(8,128)S(1)}, f32[64,1792]{1,0:T(8,128)S(1)}, u32[]{:S(2)}, u32[]{:S(2)}) collective-permute-start(f32[64,1792]{1,0:T(8,128)S(1)} %get-tuple-element.274), channel_id=1, source_target_pairs={{0,16},{8,24},{16,0},{24,8},{1,17},{9,25},{17,1},{25,9},{2,18},{10... | collective-permute-start | bytes 1376264 | tf_op jit(solution)/shard_map/ppermute | solution.py:389
  299.3 28.6 %collective-permute-start.27 = (f32[64,1792]{1,0:T(8,128)S(1)}, f32[64,1792]{1,0:T(8,128)S(1)}, u32[]{:S(2)}, u32[]{:S(2)}) collective-permute-start(f32[64,1792]{1,0:T(8,128)S(1)} %get-tuple-element.271), channel_id=1, source_target_pairs={{0,24},{8,0},{16,8},{24,16},{1,25},{9,1},{17,9},{25,17},{2,26},{10... | collective-permute-start | bytes 1376264 | tf_op jit(solution)/shard_map/ppermute | solution.py:389
  302.4 26.4 %copy-start.105 = (bf16[1024,896]{1,0:T(8,128)(2,1)S(1)}, bf16[1024,896]{1,0:T(8,128)(2,1)}, u32[]{:S(2)}) copy-start(bf16[1024,896]{1,0:T(8,128)(2,1)} %get-tuple-element.200) | copy-start | bytes 5505028
  302.4 26.3 %copy-start.45 = (bf16[1024,896]{1,0:T(8,128)(2,1)S(1)}, bf16[1024,896]{1,0:T(8,128)(2,1)}, u32[]{:S(2)}) copy-start(bf16[1024,896]{1,0:T(8,128)(2,1)} %constant_dynamic-slice_fusion.1) | copy-start | bytes 5505028
  302.4 26.3 %copy-start.55 = (bf16[256,2048]{1,0:T(8,128)(2,1)S(1)}, bf16[256,2048]{1,0:T(8,128)(2,1)}, u32[]{:S(2)}) copy-start(bf16[256,2048]{1,0:T(8,128)(2,1)} %copy-done.54) | copy-start | bytes 3145732
  313.9 14.0 %copy-start.75 = (f32[64,1792]{1,0:T(8,128)}, f32[64,1792]{1,0:T(8,128)S(1)}, u32[]{:S(2)}) copy-start(f32[64,1792]{1,0:T(8,128)S(1)} %collective-permute-done.25) | copy-start | bytes 1376260
  332.3 7.5 %collective-permute-start.30 = (f32[1024,1024]{1,0:T(8,128)}, f32[1024,1024]{1,0:T(8,128)}, u32[]{:S(2)}, u32[]{:S(2)}) collective-permute-start(f32[1024,1024]{1,0:T(8,128)} %add_add_fusion.2), channel_id=1, source_target_pairs={{0,1},{1,0},{2,3},{3,2},{4,5},{5,4},{6,7},{7,6},{8,9},{9,8},{10,11... | collective-permute-start | bytes 12582920 | tf_op jit(solution)/shard_map/ppermute | solution.py:368
  332.3 13.5 %collective-permute-start.41 = (f32[1024,1024]{1,0:T(8,128)}, f32[1024,1024]{1,0:T(8,128)}, u32[]{:S(2)}, u32[]{:S(2)}) collective-permute-start(f32[1024,1024]{1,0:T(8,128)} %get-tuple-element.235), channel_id=1, source_target_pairs={{0,1},{1,0},{2,3},{3,2},{4,5},{5,4},{6,7},{7,6},{8,9},{9,8},{10,11... | collective-permute-start | bytes 12582920 | tf_op jit(solution)/shard_map/ppermute | solution.py:368
  336.7 9.1 %copy-start.4 = (f32[512,1024]{1,0:T(8,128)S(1)}, f32[512,1024]{1,0:T(8,128)}, u32[]{:S(2)}) copy-start(f32[512,1024]{1,0:T(8,128)} %copy-done.2) | copy-start | bytes 6291460
  336.7 23.2 %collective-permute-start.28 = (f32[256,896]{1,0:T(8,128)}, f32[256,896]{1,0:T(8,128)S(1)}, u32[]{:S(2)}, u32[]{:S(2)}) collective-permute-start(f32[256,896]{1,0:T(8,128)} %fusion.44), channel_id=1, source_target_pairs={{0,4},{4,0},{1,5},{5,1},{2,6},{6,2},{3,7},{7,3},{8,12},{12,8},{9,1... | collective-permute-start | bytes 2752520 | tf_op jit(solution)/shard_map/ppermute | solution.py:368
  337.4 22.6 %collective-permute-start.29 = (f32[256,512]{1,0:T(8,128)S(1)}, f32[256,512]{1,0:T(8,128)S(1)}, u32[]{:S(2)}, u32[]{:S(2)}) collective-permute-start(f32[256,512]{1,0:T(8,128)S(1)} %copy-done.65), channel_id=1, source_target_pairs={{0,2},{2,0},{1,3},{3,1},{4,6},{6,4},{5,7},{7,5},{8,10},{10,8},{9,1... | collective-permute-start | bytes 1572872 | tf_op jit(solution)/shard_map/ppermute | solution.py:368
  339.1 15.2 %copy-start.85 = (f32[1024]{0:T(1024)S(1)}, f32[1024]{0:T(1024)}, u32[]{:S(2)}) copy-start(f32[1024]{0:T(1024)} %copy-done.84) | copy-start | bytes 12292
  360.0 38.2 %collective-permute-start.31 = (f32[512,512]{1,0:T(8,128)S(1)}, f32[512,512]{1,0:T(8,128)S(1)}, u32[]{:S(2)}, u32[]{:S(2)}) collective-permute-start(f32[512,512]{1,0:T(8,128)S(1)} %copy-done.98), channel_id=1, source_target_pairs={{0,2},{2,0},{1,3},{3,1},{4,6},{6,4},{5,7},{7,5},{8,10},{10,8},{9,1... | collective-permute-start | bytes 3145736 | tf_op jit(solution)/shard_map/ppermute | solution.py:368
  361.5 36.6 %collective-permute-start.32 = (f32[512,512]{1,0:T(8,128)S(1)}, f32[512,512]{1,0:T(8,128)S(1)}, u32[]{:S(2)}, u32[]{:S(2)}) collective-permute-start(f32[512,512]{1,0:T(8,128)S(1)} %copy-done.97), channel_id=1, source_target_pairs={{0,4},{4,0},{1,5},{5,1},{2,6},{6,2},{3,7},{7,3},{8,12},{12,8},{9,1... | collective-permute-start | bytes 3145736 | tf_op jit(solution)/shard_map/ppermute | solution.py:368
  365.0 33.1 %copy-start.21 = (bf16[512,1024]{1,0:T(8,128)(2,1)S(1)}, bf16[512,1024]{1,0:T(8,128)(2,1)}, u32[]{:S(2)}) copy-start(bf16[512,1024]{1,0:T(8,128)(2,1)} %copy-done.20) | copy-start | bytes 3145732
  365.0 33.1 %copy-start.26 = (bf16[1024,1024]{1,0:T(8,128)(2,1)S(1)}, bf16[1024,1024]{1,0:T(8,128)(2,1)}, u32[]{:S(2)}) copy-start(bf16[1024,1024]{1,0:T(8,128)(2,1)} %copy-done.24) | copy-start | bytes 6291460
  365.1 18.4 %collective-permute-start.33 = (f32[64,1408]{1,0:T(8,128)S(1)}, f32[64,1408]{1,0:T(8,128)S(1)}, u32[]{:S(2)}, u32[]{:S(2)}) collective-permute-start(f32[64,1408]{1,0:T(8,128)S(1)} %get-tuple-element.283), channel_id=1, source_target_pairs={{0,8},{8,16},{16,24},{24,0},{1,9},{9,17},{17,25},{25,1},{2,10},{10... | collective-permute-start | bytes 1081352 | tf_op jit(solution)/shard_map/ppermute | solution.py:389
  374.4 23.8 %collective-permute-start.34 = (f32[64,1408]{1,0:T(8,128)S(1)}, f32[64,1408]{1,0:T(8,128)S(1)}, u32[]{:S(2)}, u32[]{:S(2)}) collective-permute-start(f32[64,1408]{1,0:T(8,128)S(1)} %get-tuple-element.284), channel_id=1, source_target_pairs={{0,16},{8,24},{16,0},{24,8},{1,17},{9,25},{17,1},{25,9},{2,18},{10... | collective-permute-start | bytes 1081352 | tf_op jit(solution)/shard_map/ppermute | solution.py:389
  374.7 23.4 %collective-permute-start.35 = (f32[64,1408]{1,0:T(8,128)S(1)}, f32[64,1408]{1,0:T(8,128)S(1)}, u32[]{:S(2)}, u32[]{:S(2)}) collective-permute-start(f32[64,1408]{1,0:T(8,128)S(1)} %get-tuple-element.281), channel_id=1, source_target_pairs={{0,24},{8,0},{16,8},{24,16},{1,25},{9,1},{17,9},{25,17},{2,26},{10... | collective-permute-start | bytes 1081352 | tf_op jit(solution)/shard_map/ppermute | solution.py:389
  377.6 21.0 %copy-start.28 = (bf16[512,1024]{1,0:T(8,128)(2,1)S(1)}, bf16[512,1024]{1,0:T(8,128)(2,1)}, u32[]{:S(2)}) copy-start(bf16[512,1024]{1,0:T(8,128)(2,1)} %get-tuple-element.207) | copy-start | bytes 3145732
  399.1 1.2 collective-permute-start.36
  400.4 19.7 %collective-permute-start.37 = (f32[256,512]{1,0:T(8,128)S(1)}, f32[256,512]{1,0:T(8,128)S(1)}, u32[]{:S(2)}, u32[]{:S(2)}) collective-permute-start(f32[256,512]{1,0:T(8,128)S(1)} %convolution_add_fusion.5), channel_id=1, source_target_pairs={{0,4},{4,0},{1,5},{5,1},{2,6},{6,2},{3,7},{7,3},{8,12},{12,8},{9,1... | collective-permute-start | bytes 1572872 | tf_op jit(solution)/shard_map/ppermute | solution.py:368
  401.6 18.4 %collective-permute-start.38 = (f32[256,512]{1,0:T(8,128)S(1)}, f32[256,512]{1,0:T(8,128)S(1)}, u32[]{:S(2)}, u32[]{:S(2)}) collective-permute-start(f32[256,512]{1,0:T(8,128)S(1)} %convolution_add_fusion.2), channel_id=1, source_target_pairs={{0,2},{2,0},{1,3},{3,1},{4,6},{6,4},{5,7},{7,5},{8,10},{10,8},{9,1... | collective-permute-start | bytes 1572872 | tf_op jit(solution)/shard_map/ppermute | solution.py:368
  402.5 13.6 %collective-permute-start.39 = (f32[8,1024]{1,0:T(8,128)S(1)}, f32[8,1024]{1,0:T(8,128)S(1)}, u32[]{:S(2)}, u32[]{:S(2)}) collective-permute-start(f32[8,1024]{1,0:T(8,128)S(1)} %select_maximum_fusion), channel_id=1, source_target_pairs={{0,2},{2,0},{1,3},{3,1},{4,6},{6,4},{5,7},{7,5},{8,10},{10,8},{9,1... | collective-permute-start | bytes 98312 | tf_op jit(solution)/shard_map/ppermute | solution.py:368
  416.1 3.9 collective-permute-start.40
  420.0 16.3 %collective-permute-start.44 = (f32[8,1024]{1,0:T(8,128)S(1)}, f32[8,1024]{1,0:T(8,128)S(1)}, u32[]{:S(2)}, u32[]{:S(2)}) collective-permute-start(f32[8,1024]{1,0:T(8,128)S(1)} %add.429), channel_id=1, source_target_pairs={{0,24},{8,0},{16,8},{24,16},{1,25},{9,1},{17,9},{25,17},{2,26},{10... | collective-permute-start | bytes 98312 | tf_op jit(solution)/shard_map/ppermute | solution.py:501
  430.2 6.1 %collective-permute-start.43 = (f32[8,1024]{1,0:T(8,128)S(1)}, f32[8,1024]{1,0:T(8,128)S(1)}, u32[]{:S(2)}, u32[]{:S(2)}) collective-permute-start(f32[8,1024]{1,0:T(8,128)S(1)} %add.429), channel_id=1, source_target_pairs={{0,16},{8,24},{16,0},{24,8},{1,17},{9,25},{17,1},{25,9},{2,18},{10... | collective-permute-start | bytes 98312 | tf_op jit(solution)/shard_map/ppermute | solution.py:501
  430.2 6.1 %collective-permute-start.42 = (f32[8,1024]{1,0:T(8,128)S(1)}, f32[8,1024]{1,0:T(8,128)S(1)}, u32[]{:S(2)}, u32[]{:S(2)}) collective-permute-start(f32[8,1024]{1,0:T(8,128)S(1)} %add.429), channel_id=1, source_target_pairs={{0,8},{8,16},{16,24},{24,0},{1,9},{9,17},{17,25},{25,1},{2,10},{10... | collective-permute-start | bytes 98312 | tf_op jit(solution)/shard_map/ppermute | solution.py:501
  431.9 10.0 %collective-permute-start.47 = (f32[64,1024]{1,0:T(8,128)S(1)}, f32[64,1024]{1,0:T(8,128)S(1)}, u32[]{:S(2)}, u32[]{:S(2)}) collective-permute-start(f32[64,1024]{1,0:T(8,128)S(1)} %get-tuple-element.286), channel_id=1, source_target_pairs={{0,24},{8,0},{16,8},{24,16},{1,25},{9,1},{17,9},{25,17},{2,26},{10... | collective-permute-start | bytes 786440 | tf_op jit(solution)/shard_map/ppermute | solution.py:389
  435.2 21.9 %collective-permute-start.46 = (f32[64,1024]{1,0:T(8,128)S(1)}, f32[64,1024]{1,0:T(8,128)S(1)}, u32[]{:S(2)}, u32[]{:S(2)}) collective-permute-start(f32[64,1024]{1,0:T(8,128)S(1)} %get-tuple-element.287), channel_id=1, source_target_pairs={{0,16},{8,24},{16,0},{24,8},{1,17},{9,25},{17,1},{25,9},{2,18},{10... | collective-permute-start | bytes 786440 | tf_op jit(solution)/shard_map/ppermute | solution.py:389
  436.3 20.8 %collective-permute-start.45 = (f32[64,1024]{1,0:T(8,128)S(1)}, f32[64,1024]{1,0:T(8,128)S(1)}, u32[]{:S(2)}, u32[]{:S(2)}) collective-permute-start(f32[64,1024]{1,0:T(8,128)S(1)} %get-tuple-element.285), channel_id=1, source_target_pairs={{0,8},{8,16},{16,24},{24,0},{1,9},{9,17},{17,25},{25,1},{2,10},{10... | collective-permute-start | bytes 786440 | tf_op jit(solution)/shard_map/ppermute | solution.py:389
  (91 other events, 368.1 us)
